TPU v7x, 32 devices: a whole 2x2x4 slice. The times are simulated.
32 devices in a mesh: grp: 2 (over x), pop: 2 (over core), mp: 8 (over z, y).
Axes of the slice: x: 2, y: 2, z: 4, core: 2. Of those that a mesh axis runs over, the one named last changes fastest.
Arguments:
- token_ids: int32 [1024, 2], P('grp'), parts along dimension 0, may hold values from 0 to 32767
- ranks: int32 [1024], P(('grp', 'pop')), parts along dimension 0, may hold values from 0 to 511, each once
- embedding: bfloat16 [32768, 4096], P('pop', 'mp'), may hold values from -6 to 6
- mix_key: float32 [4096], P('mp'), may hold values from 0.05 to 0.95
- key_weight: bfloat16 [4096, 16384], P('pop', 'mp'), may hold values from -6 to 6
- value_weight: bfloat16 [16384, 4096], P('mp', 'pop'), may hold values from -6 to 6
- key_left: bfloat16 [1024, 4096], P(('grp', 'pop'), 'mp'), parts along dimension 0, may hold values from -6 to 6
- key_right: bfloat16 [1024, 16384], P(('grp', 'pop'), 'mp'), parts along dimension 0, may hold values from -6 to 6
- value_left: bfloat16 [1024, 16384], P(('grp', 'pop'), 'mp'), parts along dimension 0, may hold values from -6 to 6
- value_right: bfloat16 [1024, 4096], P(('grp', 'pop'), 'mp'), parts along dimension 0, may hold values from -6 to 6
Outputs:
- mixed: bfloat16 [2048, 4096], P(('grp', 'pop'), 'mp'), parts along dimension 0
- new_key: bfloat16 [8192, 16384], P(('grp', 'pop'), 'mp'), parts along dimension 0
- new_value: bfloat16 [32768, 4096], P(('grp', 'mp'), 'pop'), parts along dimension 0
There are 2 independent parts, one for each index of `grp`. A program takes and returns all parts, laid end to end along the dimension named above; an argument that names none is the same for every part. Nothing has to cross between parts.
Inputs may be any that keep to these rules, and one draw needn't show every extreme that they name: `ranks`: each member's rank; every rank appears exactly once in a run. `token_ids`: token ids index the embedding table.
All inputs are finite; a program needn't handle non-finite values.
Results may differ from a plain program's by a relative error of at most 0.006.
Values may be sent and summed in bfloat16 or wider, within the bound.
A program may use at most 320 MiB of HBM per device.

v0:
```python
import jax
import jax.numpy as jnp
from jax import lax
from jax.sharding import PartitionSpec as P

D = 4096
FF = 16384


noise_scale = 0.5
step_scale = 8.0


def contract_first(left, right):
    return lax.dot_general(
        left, right, (((0,), (0,)), ((), ())), preferred_element_type=jnp.float32
    )


def shards(
    token_ids,
    ranks,
    embedding,
    mix_key,
    key_weight,
    value_weight,
    key_left,
    key_right,
    value_left,
    value_right,
):
    members = ranks.shape[0]
    population = members * lax.axis_size("pop")
    half_vocab = embedding.shape[0]
    local_ids = token_ids.reshape(-1) - lax.axis_index("pop") * half_vocab
    inside = (local_ids >= 0) & (local_ids < half_vocab)
    looked = jnp.take(embedding, jnp.clip(local_ids, 0, half_vocab - 1), axis=0)
    picked = jnp.where(inside[:, None], looked.astype(jnp.float32), 0.0)
    own_rows = lax.psum_scatter(
        picked.astype(jnp.bfloat16), "pop", scatter_dimension=0, tiled=True
    ).astype(jnp.float32)
    local_width = own_rows.shape[1]
    rows3 = own_rows.reshape(members, 2, local_width)
    before = jnp.concatenate(
        [jnp.zeros((members, 1, local_width), jnp.float32), rows3[:, :1]], axis=1
    )
    keyed = (
        (rows3 + (before - rows3) * mix_key).astype(jnp.bfloat16).reshape(members * 2, local_width)
    )
    keyed_full, left_full, right_full = (
        lax.all_gather(keyed, "mp", axis=1, tiled=True),
        lax.all_gather(key_left, "mp", axis=1, tiled=True),
        lax.all_gather(value_right, "mp", axis=1, tiled=True),
    )
    inv_model = D ** (-0.5)
    inv_hidden = FF ** (-0.5)
    projected = jnp.dot(
        keyed_full,
        lax.all_gather(key_weight, "pop", axis=0, tiled=True),
        preferred_element_type=jnp.float32,
    )
    inner_key = jnp.einsum(
        "mtd,md->mt",
        keyed_full.reshape(members, 2, D),
        left_full,
        preferred_element_type=jnp.float32,
    )
    hidden = (
        projected.reshape(members, 2, -1) * inv_model
        + noise_scale
        * inv_model
        * inner_key[:, :, None]
        * key_right.astype(jnp.float32)[:, None, :]
    )
    squared = (jnp.maximum(hidden, 0.0) ** 2).astype(jnp.bfloat16)
    inner_value = jnp.einsum(
        "mtf,mf->mt", squared, value_left, preferred_element_type=jnp.float32
    ).reshape(-1)
    flat_squared = squared.reshape(members * 2, -1)
    piece = lax.all_gather(value_weight, "pop", axis=1, tiled=True)
    count = piece.shape[1]
    spread = (
        jnp.broadcast_to(right_full[:, None, :], (members, 2, count))
        .reshape(members * 2, count)
        .astype(jnp.float32)
    )
    terms = (
        jnp.dot(flat_squared, piece, preferred_element_type=jnp.float32)
        + noise_scale * inner_value[:, None] * spread
    )
    mixed = (lax.psum_scatter(terms, "mp", scatter_dimension=1, tiled=True) * inv_hidden).astype(
        jnp.bfloat16
    )
    fitness = (2 * ranks - (population - 1)).astype(jnp.float32) / (population - 1)
    scaled_right = (fitness[:, None] * key_right.astype(jnp.float32)).astype(jnp.bfloat16)
    scaled_left = (fitness[:, None] * value_left.astype(jnp.float32)).astype(jnp.bfloat16)
    key_grad = lax.psum_scatter(
        contract_first(left_full, scaled_right), "pop", scatter_dimension=0, tiled=True
    )
    value_term = contract_first(scaled_left, right_full)
    value_grad = lax.psum_scatter(value_term, "pop", scatter_dimension=1, tiled=True)
    step = step_scale / population
    new_key = (key_weight.astype(jnp.float32) + step * key_grad).astype(jnp.bfloat16)
    new_value = (value_weight.astype(jnp.float32) + step * value_grad).astype(jnp.bfloat16)
    return (mixed, new_key, new_value)


def solution(mesh):
    placed = (
        P("grp", None),
        P(("grp", "pop")),
        P("pop", "mp"),
        P("mp"),
        P("pop", "mp"),
        P("mp", "pop"),
        P(("grp", "pop"), "mp"),
        P(("grp", "pop"), "mp"),
        P(("grp", "pop"), "mp"),
        P(("grp", "pop"), "mp"),
    )
    return jax.shard_map(
        shards,
        mesh=mesh,
        in_specs=placed,
        out_specs=(P(("grp", "pop"), "mp"), P(("grp", "pop"), "mp"), P(("grp", "mp"), "pop")),
        check_vma=False,
    )
```

profile of v0, /device:TPU:0, one launch (start us, length us, event | category | flops | bytes accessed | tf_op | source)
XLA Modules:
  0.0 562.3 jit_solution(650820236324022587)
XLA Ops:
  10.4 11.9 %gather_fusion = bf16[1024,512]{1,0:T(8,128)(2,1)S(1)} fusion(bf16[16384,512]{1,0:T(8,128)(2,1)} %param.12, s32[1024]{0:T(1024)S(1)} %broadcast_clamp_fusion), kind=kCustom, calls=%fused_computation | custom fusion | bytes 2101248 | tf_op jit(solution)/shard_map/jit(_take)/gather | solution.py:37
  24.6 10.8 %reduce-scatter.5.cloned.1.call-done = bf16[512,512]{1,0:T(8,128)(2,1)} async-done(((bf16[1024,512]{1,0:T(8,128)(2,1)}), bf16[512,512]{1,0:T(8,128)(2,1)}) %reduce-scatter.5.cloned.1.call-update) | async-done | bytes 524304 | tf_op jit(solution)/shard_map/reduce_scatter | solution.py:39
  52.6 27.2 %all-gather.14.cloned.1.call-done = bf16[256,4096]{1,0:T(8,128)(2,1)} async-done(((bf16[256,512]{1,0:T(8,128)(2,1)}), bf16[256,4096]{1,0:T(8,128)(2,1)}) %all-gather.14.cloned.1.call-update) | async-done | bytes 2097168 | tf_op jit(solution)/shard_map/all_gather | solution.py:53
  79.8 8.2 %broadcast_in_dim.39 = f32[256,2,4096]{2,1,0:T(2,128)} broadcast(bf16[256,4096]{1,0:T(8,128)(2,1)} %all-gather.14.cloned.1.call-done), dimensions={0,2} | broadcast | bytes 10485760 | tf_op jit(solution)/shard_map/broadcast_in_dim | solution.py:83
  88.0 10.9 %convert_element_type.61 = f32[512,4096]{1,0:T(8,128)} reshape(f32[256,2,4096]{2,1,0:T(2,128)} %broadcast_in_dim.39) | data formatting | bytes 16777216 | tf_op jit(solution)/shard_map/convert_element_type | solution.py:85
  98.9 56.5 %all-gather.6.cloned.1.call-done = bf16[512,4096]{1,0:T(8,128)(2,1)} async-done(((bf16[512,512]{1,0:T(8,128)(2,1)}), bf16[512,4096]{1,0:T(8,128)(2,1)}) %all-gather.6.cloned.1.call-update) | async-done | bytes 4194320 | tf_op jit(solution)/shard_map/all_gather | solution.py:51
  155.4 7.6 %reshape.95 = bf16[256,2,4096]{2,1,0:T(2,128)(2,1)} reshape(bf16[512,4096]{1,0:T(8,128)(2,1)} %all-gather.6.cloned.1.call-done) | data formatting | bytes 8388608 | tf_op jit(solution)/shard_map/reshape | solution.py:64
  163.0 43.3 %all-gather.10.cloned.1.call-done = bf16[256,4096]{1,0:T(8,128)(2,1)} async-done(((bf16[256,512]{1,0:T(8,128)(2,1)}), bf16[256,4096]{1,0:T(8,128)(2,1)}) %all-gather.10.cloned.1.call-update) | async-done | bytes 2097168 | tf_op jit(solution)/shard_map/all_gather | solution.py:52
  206.3 10.5 %fusion = f32[256,1,2]{2,1,0:T(1,128)S(1)} fusion(bf16[256,2,4096]{2,1,0:T(2,128)(2,1)} %reshape.95, bf16[256,4096,1]{1,0,2:T(8,128)(2,1)} %bitcast.15), kind=kOutput, calls=%fused_computation.7 | convolution fusion | flops 4194304 | bytes 6293504 | tf_op jit(solution)/shard_map/mtd,md->mt/dot_general | solution.py:62
  216.9 19.1 %all-gather.8.cloned.1.call-done = bf16[4096,2048]{1,0:T(8,128)(2,1)} async-done(((bf16[2048,2048]{1,0:T(8,128)(2,1)}), bf16[4096,2048]{1,0:T(8,128)(2,1)}) %all-gather.8.cloned.1.call-update) | async-done | bytes 16777232 | tf_op jit(solution)/shard_map/all_gather | solution.py:59
  236.1 14.9 %convolution_multiply_fusion = f32[512,2048]{1,0:T(8,128)} fusion(bf16[512,4096]{1,0:T(8,128)(2,1)} %all-gather.6.cloned.1.call-done, bf16[4096,2048]{1,0:T(8,128)(2,1)} %all-gather.8.cloned.1.call-done), kind=kOutput, calls=%fused_computation.9 | convolution fusion | flops 8590983168 | bytes 25165824 | tf_op jit(solution)/shard_map/dot_general | solution.py:57
  257.4 9.1 %fusion.4 = f32[256,1,2]{2,1,0:T(1,128)S(1)} fusion(bf16[256,2048,1]{1,0,2:T(8,128)(2,1)} %bitcast.16, f32[256,2,2048]{2,1,0:T(2,128)} %mul.116, f32[256,2]{1,0:T(8,128)S(1)} %broadcast_multiply_fusion.1, f32[256,2048]{1,0:T(8,128)S(1)} %convert_element_type.57), kind=kOutput, calls=%fused_computation.15 | convolution fusion | flops 7340032 | bytes 7344128 | tf_op jit(solution)/shard_map/mtf,mf->mt/dot_general | solution.py:76
  268.9 18.1 %multiply_add_fusion = f32[512,4096]{1,0:T(8,128)} fusion(f32[512,4096]{1,0:T(8,128)} %convert_element_type.61, bf16[2048,4096]{1,0:T(8,128)(2,1)} %all-gather.12.cloned.1.call-done, f32[512]{0:T(512)S(1)} %mul.121, f32[512,2048]{1,0:T(8,128)} %convolution_multiply_fusion, f32[512,2048]{1,0:T(8,128)} %mul.114, f32[512]{0:T(512)S(1)} %mul.111), kind=kOutput, calls=%fused_computation.4 | convolution fusion | flops 8599371776 | bytes 41947136 | tf_op jit(solution)/shard_map/dot_general | solution.py:88
  288.7 13.8 %convolution_bitcast_fusion = f32[4096,2048]{0,1:T(8,128)} fusion(bf16[256,4096]{1,0:T(8,128)(2,1)S(1)} %copy-done.2, f32[256]{0:T(256)S(1)} %convert_multiply_fusion, bf16[256,2048]{1,0:T(8,128)(2,1)S(1)} %copy-done), kind=kOutput, calls=%fused_computation.1 | convolution fusion | flops 4296540160 | bytes 36701184 | tf_op jit(solution)/shard_map/dot_general | solution.py:15
  304.4 13.4 %fusion.6 = f32[2048,4096]{0,1:T(8,128)} fusion(bf16[256,4096]{1,0:T(8,128)(2,1)S(1)} %copy-done.1, bf16[256,2048]{1,0:T(8,128)(2,1)S(1)} %copy-done.3, f32[256]{0:T(256)S(1)} %convert_multiply_fusion), kind=kOutput, calls=%fused_computation.17 | convolution fusion | flops 4296540160 | bytes 36701184 | tf_op jit(solution)/shard_map/dot_general | solution.py:15
  317.8 12.3 %copy.21 = bf16[2048,2048]{0,1:T(8,128)(2,1)} copy(bf16[2048,2048]{1,0:T(8,128)(2,1)} %param.14) | data formatting | bytes 16777216 | tf_op args[4]
  330.1 12.4 %copy.22 = bf16[2048,2048]{0,1:T(8,128)(2,1)} copy(bf16[2048,2048]{1,0:T(8,128)(2,1)} %param.15) | data formatting | bytes 16777216 | tf_op args[5]
  342.5 93.3 %reduce-scatter.7.cloned.1.call-done = f32[512,512]{1,0:T(8,128)} async-done(((f32[512,4096]{1,0:T(8,128)}), f32[512,512]{1,0:T(8,128)}) %reduce-scatter.7.cloned.1.call-update) | async-done | bytes 1048592 | tf_op jit(solution)/shard_map/reduce_scatter | solution.py:91
  437.9 44.2 %reduce-scatter.9.cloned.1.call-done = f32[2048,2048]{0,1:T(8,128)} async-done(((f32[4096,2048]{0,1:T(8,128)}), f32[2048,2048]{0,1:T(8,128)}) %reduce-scatter.9.cloned.1.call-update) | async-done | bytes 16777232 | tf_op jit(solution)/shard_map/reduce_scatter | solution.py:97
  482.1 12.2 %add_convert_fusion.1 = bf16[2048,2048]{0,1:T(8,128)(2,1)} fusion(f32[2048,2048]{0,1:T(8,128)} %reduce-scatter.9.cloned.1.call-done, bf16[2048,2048]{0,1:T(8,128)(2,1)} %copy.21), kind=kLoop, calls=%fused_computation.3 | loop fusion | flops 16777216 | bytes 33554432 | tf_op jit(solution)/shard_map/convert_element_type | solution.py:103
  494.3 13.4 %copy.24 = bf16[2048,2048]{1,0:T(8,128)(2,1)} copy(bf16[2048,2048]{0,1:T(8,128)(2,1)} %add_convert_fusion.1) | data formatting | bytes 16777216
  507.7 22.9 %reduce-scatter.11.cloned.1.call-done = f32[2048,2048]{0,1:T(8,128)} async-done(((f32[2048,4096]{0,1:T(8,128)}), f32[2048,2048]{0,1:T(8,128)}) %reduce-scatter.11.cloned.1.call-update) | async-done | bytes 16777232 | tf_op jit(solution)/shard_map/reduce_scatter | solution.py:101
  530.6 12.0 %add_convert_fusion = bf16[2048,2048]{0,1:T(8,128)(2,1)} fusion(f32[2048,2048]{0,1:T(8,128)} %reduce-scatter.11.cloned.1.call-done, bf16[2048,2048]{0,1:T(8,128)(2,1)} %copy.22), kind=kLoop, calls=%fused_computation.2 | loop fusion | flops 16777216 | bytes 33554432 | tf_op jit(solution)/shard_map/convert_element_type | solution.py:104
  542.6 12.2 %copy.25 = bf16[2048,2048]{1,0:T(8,128)(2,1)} copy(bf16[2048,2048]{0,1:T(8,128)(2,1)} %add_convert_fusion) | data formatting | bytes 16777216
  (56 shorter events, 36.3 us)
Async XLA Ops:
  8.0 27.4 %reduce-scatter.5.cloned.1.call-start = ((), (), s32[]{:S(2)}) async-start(), calls=%async_computation.4 | async-start | bytes 1572864 | tf_op jit(solution)/shard_map/reduce_scatter | solution.py:39
  22.3 15.2 %copy-start.4 = (f32[512]{0:T(512)S(1)}, f32[512]{0:T(512)}, u32[]{:S(2)}) copy-start(f32[512]{0:T(512)} %param.13) | copy-start | bytes 6148
  24.0 55.8 %all-gather.14.cloned.1.call-start = ((), (), s32[]{:S(2)}) async-start(), calls=%async_computation.9 | async-start | bytes 2359296 | tf_op jit(solution)/shard_map/all_gather | solution.py:53
  24.6 130.8 %all-gather.6.cloned.1.call-start = ((), (), s32[]{:S(2)}) async-start(), calls=%async_computation.5 | async-start | bytes 4718592 | tf_op jit(solution)/shard_map/all_gather | solution.py:51
  39.5 166.7 %all-gather.10.cloned.1.call-start = ((), (), s32[]{:S(2)}) async-start(), calls=%async_computation.7 | async-start | bytes 2359296 | tf_op jit(solution)/shard_map/all_gather | solution.py:52
  40.1 196.0 %all-gather.8.cloned.1.call-start = ((), (), s32[]{:S(2)}) async-start(), calls=%async_computation.6 | async-start | bytes 25165824 | tf_op jit(solution)/shard_map/all_gather | solution.py:59
  40.8 1.2 copy-start
  40.8 228.1 %all-gather.12.cloned.1.call-start = ((), (), s32[]{:S(2)}) async-start(), calls=%async_computation.8 | async-start | bytes 25165824 | tf_op jit(solution)/shard_map/all_gather | solution.py:80
  41.6 394.2 %reduce-scatter.7.cloned.1.call-start = ((), (), s32[]{:S(2)}) async-start(), calls=%async_computation.10 | async-start | bytes 9437184 | tf_op jit(solution)/shard_map/reduce_scatter | solution.py:91
  287.0 0.7 copy-start.5
  287.0 1.6 copy-start.2
  287.1 195.0 %reduce-scatter.9.cloned.1.call-start = ((), (), s32[]{:S(2)}) async-start(), calls=%async_computation.11 | async-start | bytes 50331648 | tf_op jit(solution)/shard_map/reduce_scatter | solution.py:97
  302.5 1.6 copy-start.1
  302.5 1.9 copy-start.3
  302.5 228.1 %reduce-scatter.11.cloned.1.call-start = ((), (), s32[]{:S(2)}) async-start(), calls=%async_computation.12 | async-start | bytes 50331648 | tf_op jit(solution)/shard_map/reduce_scatter | solution.py:101
Sparse Core Ops, SparseCore 0:
  24.1 11.2 reduce-scatter.4
Sparse Core Ops, SparseCore 1:
  26.5 53.2 all-gather.13
  82.4 72.9 all-gather.5
  157.5 48.7 all-gather.9
  207.9 28.1 all-gather.7
  237.7 31.1 all-gather.11
  287.2 148.6 reduce-scatter.6
  437.9 44.1 reduce-scatter.8
  484.2 46.3 reduce-scatter.10
where the time goes:
time: 565 us; the launch traced here: 562 us
  waiting for transfers between devices  322 us (57%)
  local copies, waits for them, and re-layouts  113 us (20%)
  matrix products  79.8 us (14%)
  other arithmetic  30.7 us (5%)
  between operations  15.7 us (3%)
    reduce_scatter x1, waiting for transfers between devices, shards(): lax.psum_scatter(terms, 'mp', scatter_dimension=1, tiled=True) * inv_hidden  93.3 us
    all_gather x1, waiting for transfers between devices, shards(): lax.all_gather(keyed, 'mp', axis=1, tiled=True)  56.5 us
    unnamed x16, local copies, waits for them, and re-layouts  53.9 us
    reduce_scatter x1, waiting for transfers between devices, shards(): lax.psum_scatter(contract_first(left_full, scaled_right), 'pop', scatter_...  44.2 us
    all_gather x1, waiting for transfers between devices, shards(): lax.all_gather(key_left, 'mp', axis=1, tiled=True)  43.3 us
    dot_general x2, matrix products, contract_first(): lax.dot_general(left, right, (((0,), (0,)), ((), ())), preferred_element_...  27.2 us
    all_gather x1, waiting for transfers between devices, shards(): lax.all_gather(value_right, 'mp', axis=1, tiled=True)  27.2 us
    reduce_scatter x1, waiting for transfers between devices, shards(): lax.psum_scatter(value_term, 'pop', scatter_dimension=1, tiled=True)  22.9 us
  transfers between devices with their start and end apart: 9, of which 9 were waited for; matrix products, arithmetic and copies ran while one was open for 29% of the time, Pallas kernels for 0%

commit v1 on v0

v1 whole, which is shorter than its diff:
```python
import functools

import jax
import jax.numpy as jnp
from jax import lax
from jax.experimental import pallas as pl
from jax.experimental.pallas import tpu as pltpu
from jax.sharding import PartitionSpec as P

noise_scale = 0.5
step_scale = 8.0
vmem_bytes = 58 * 1024 * 1024
pad_rows = 16


def dot(left, right):
    return jnp.dot(left, right, preferred_element_type=jnp.float32)


def contract_first(left, right):
    return lax.dot_general(
        left, right, (((0,), (0,)), ((), ())), preferred_element_type=jnp.float32
    )


def forward_kernel(
    inv_model, inv_hidden, side_ref, keyed_ref, key_own, key_peer, value_own, value_peer,
    key_right, value_left, value_right, out_ref, total, inner_key, inner_value,
):
    step, last = pl.program_id(0), pl.num_programs(0) - 1
    slices, padded, width = keyed_ref.shape
    tokens, half = padded - pad_rows, slices // 2
    tile = key_own.shape[1]
    mine = side_ref[0] * half
    theirs = half - mine

    @pl.when(step == 0)
    def _():
        groups = tokens // width
        line = lax.broadcasted_iota(jnp.int32, (pad_rows, 128), 0)
        for g in range(groups):
            chosen = (line < 3 * groups) & (line % groups == g)
            ones = jnp.where(chosen, 1.0, 0.0).astype(jnp.bfloat16)
            partial = jnp.zeros((width, 128), jnp.float32)
            for s in range(slices):
                partial += contract_first(keyed_ref[s, tokens:, :], ones)
            inner_key[g * width : (g + 1) * width, :] = partial * (noise_scale * inv_model)
        inner_value[...] = jnp.zeros_like(inner_value)

    projected = jnp.zeros((tokens, tile), jnp.float32)
    for j in range(half):
        rows = slice(j * width, (j + 1) * width)
        projected += dot(keyed_ref[mine + j, :tokens, :], key_own[rows, :])
        projected += dot(keyed_ref[theirs + j, :tokens, :], key_peer[rows, :])
    right = key_right[...].astype(jnp.float32)
    left = value_left[...].astype(jnp.float32)
    members = right.shape[0]
    parts = []
    for t in range(tokens // members):
        own = slice(t * members, (t + 1) * members)
        pieces = []
        for c in range(0, tile, 128):
            cols = slice(c, c + 128)
            hidden = projected[own, cols] * inv_model + inner_key[own, :] * right[:, cols]
            rounded = (jnp.maximum(hidden, 0.0) ** 2).astype(jnp.bfloat16)
            inner_value[own, :] += rounded.astype(jnp.float32) * left[:, cols]
            pieces.append(rounded)
        parts.append(jnp.concatenate(pieces, axis=1))
    squared = jnp.concatenate(parts, axis=0)

    for j in range(half):
        cols = slice(j * width, (j + 1) * width)
        for base, weight in ((mine, value_own), (theirs, value_peer)):
            product = dot(squared, weight[:, cols])

            @pl.when(step == 0)
            def _():
                total[base + j] = product

            @pl.when(step > 0)
            def _():
                total[base + j] += product

    @pl.when(step == last)
    def _():
        amount = noise_scale * jnp.sum(inner_value[...], axis=1, keepdims=True)
        for s in range(slices):
            spread = value_right[s].astype(jnp.float32)
            for t in range(tokens // members):
                own = slice(t * members, (t + 1) * members)
                out_ref[s, own, :] = (
                    (total[s, own, :] + amount[own, :] * spread) * inv_hidden
                ).astype(jnp.bfloat16)


def forward(side, keyed, key_own, key_peer, value_own, value_peer, key_right, value_left,
            value_right, inv_model, inv_hidden):
    slices, padded, width = keyed.shape
    tokens = padded - pad_rows
    rows, hidden = key_own.shape
    members = key_right.shape[0]
    tile = min(512, hidden)
    whole = lambda i, s: (0, 0, 0)
    column = lambda i, s: (0, i)
    row = lambda i, s: (i, 0)
    return pl.pallas_call(
        functools.partial(forward_kernel, inv_model, inv_hidden),
        out_shape=jax.ShapeDtypeStruct((slices, tokens, width), jnp.bfloat16),
        grid_spec=pltpu.PrefetchScalarGridSpec(
            num_scalar_prefetch=1,
            grid=(hidden // tile,),
            in_specs=[
                pl.BlockSpec(keyed.shape, whole),
                pl.BlockSpec((rows, tile), column),
                pl.BlockSpec((rows, tile), column),
                pl.BlockSpec((tile, rows), row),
                pl.BlockSpec((tile, rows), row),
                pl.BlockSpec((members, tile), column),
                pl.BlockSpec((members, tile), column),
                pl.BlockSpec(value_right.shape, whole),
            ],
            out_specs=pl.BlockSpec((slices, tokens, width), whole),
            scratch_shapes=[
                pltpu.VMEM((slices, tokens, width), jnp.float32),
                pltpu.VMEM((tokens, 128), jnp.float32),
                pltpu.VMEM((tokens, 128), jnp.float32),
            ],
        ),
        compiler_params=pltpu.CompilerParams(vmem_limit_bytes=vmem_bytes),
        cost_estimate=pl.CostEstimate(
            flops=8 * tokens * rows * hidden,
            bytes_accessed=8 * rows * hidden + 4 * tokens * slices * width,
            transcendentals=0,
        ),
        name="forward",
    )(side, keyed, key_own, key_peer, value_own, value_peer, key_right, value_left, value_right)


def key_step_kernel(step, side_ref, left_own, left_peer, right_own, right_peer, weight, out_ref):
    columns = out_ref.shape[1]
    chunk = min(512, columns)
    own, peer = left_own[0], left_peer[0]
    for c in range(0, columns, chunk):
        cols = slice(c, c + chunk)
        grad = contract_first(own, right_own[:, cols]) + contract_first(peer, right_peer[:, cols])
        out_ref[:, cols] = (weight[:, cols].astype(jnp.float32) + step * grad).astype(jnp.bfloat16)


def key_step(side, left_all, left_peer, right_own, right_peer, weight, step):
    half, members, width = left_peer.shape
    rows, columns = weight.shape
    fixed = pl.BlockSpec((members, columns), lambda j, s: (0, 0))
    tile = pl.BlockSpec((width, columns), lambda j, s: (j, 0))
    return pl.pallas_call(
        functools.partial(key_step_kernel, step),
        out_shape=jax.ShapeDtypeStruct(weight.shape, jnp.bfloat16),
        grid_spec=pltpu.PrefetchScalarGridSpec(
            num_scalar_prefetch=1,
            grid=(half,),
            in_specs=[
                pl.BlockSpec((1, members, width), lambda j, s: (s[0] * half + j, 0, 0)),
                pl.BlockSpec((1, members, width), lambda j, s: (j, 0, 0)),
                fixed,
                fixed,
                tile,
            ],
            out_specs=tile,
        ),
        compiler_params=pltpu.CompilerParams(vmem_limit_bytes=vmem_bytes),
        cost_estimate=pl.CostEstimate(
            flops=4 * members * rows * columns,
            bytes_accessed=4 * rows * columns + 4 * members * (rows + columns),
            transcendentals=0,
        ),
        name="key_step",
    )(side, left_all, left_peer, right_own, right_peer, weight)


def value_step_kernel(step, side_ref, left_own, left_peer, right_all, right_peer, weight, out_ref):
    half, _, width = right_peer.shape
    mine = side_ref[0] * half
    own, peer = left_own[...], left_peer[...]
    for j in range(half):
        cols = slice(j * width, (j + 1) * width)
        grad = contract_first(own, right_all[mine + j]) + contract_first(peer, right_peer[j])
        out_ref[:, cols] = (weight[:, cols].astype(jnp.float32) + step * grad).astype(jnp.bfloat16)


def value_step(side, left_own, left_peer, right_all, right_peer, weight, step):
    half, members, width = right_peer.shape
    rows, columns = weight.shape
    size = min(512, rows)
    side_tile = pl.BlockSpec((members, size), lambda i, s: (0, i))
    tile = pl.BlockSpec((size, columns), lambda i, s: (i, 0))
    return pl.pallas_call(
        functools.partial(value_step_kernel, step),
        out_shape=jax.ShapeDtypeStruct(weight.shape, jnp.bfloat16),
        grid_spec=pltpu.PrefetchScalarGridSpec(
            num_scalar_prefetch=1,
            grid=(rows // size,),
            in_specs=[
                side_tile,
                side_tile,
                pl.BlockSpec(right_all.shape, lambda i, s: (0, 0, 0)),
                pl.BlockSpec(right_peer.shape, lambda i, s: (0, 0, 0)),
                tile,
            ],
            out_specs=tile,
        ),
        compiler_params=pltpu.CompilerParams(vmem_limit_bytes=vmem_bytes),
        cost_estimate=pl.CostEstimate(
            flops=4 * members * rows * columns,
            bytes_accessed=4 * rows * columns + 4 * members * (rows + columns),
            transcendentals=0,
        ),
        name="value_step",
    )(side, left_own, left_peer, right_all, right_peer, weight)


def shards(
    token_ids, ranks, embedding, mix_key, key_weight, value_weight,
    key_left, key_right, value_left, value_right,
):
    members = ranks.shape[0]
    population = members * lax.axis_size("pop")
    side = lax.axis_index("pop")
    side_ref = side.astype(jnp.int32).reshape(1)
    slices = lax.axis_size("mp")
    half = slices // 2
    width = embedding.shape[1]
    model = slices * width
    hidden = slices * key_weight.shape[1]
    swap = lambda array: lax.ppermute(array, "pop", [(0, 1), (1, 0)])

    half_vocab = embedding.shape[0]
    by_side = jnp.swapaxes(token_ids.reshape(2, members, 2), 1, 2)

    def look(which):
        ids = lax.dynamic_index_in_dim(by_side, which, 0, keepdims=False).reshape(-1)
        ids = ids - side * half_vocab
        inside = (ids >= 0) & (ids < half_vocab)
        return jnp.take(embedding, jnp.clip(ids, 0, half_vocab - 1), axis=0, mode="clip"), inside

    theirs, _ = look(1 - side)
    received = swap(theirs)
    mine, inside = look(side)
    rows = jnp.where(inside[:, None], mine, received).astype(jnp.float32)
    first, second = rows[:members], rows[members:]
    keyed = jnp.concatenate(
        [first + (0.0 - first) * mix_key, second + (first - second) * mix_key], axis=0
    ).astype(jnp.bfloat16)
    left = key_left.astype(jnp.float32)
    inner = jnp.sum(
        keyed.astype(jnp.float32).reshape(2, members, width) * left[None], axis=2
    ).reshape(-1)
    high = inner.astype(jnp.bfloat16)
    rest = inner - high.astype(jnp.float32)
    middle = rest.astype(jnp.bfloat16)
    low = (rest - middle.astype(jnp.float32)).astype(jnp.bfloat16)
    groups = -(-2 * members // width)
    tail = jnp.stack([high, middle, low]).reshape(3 * groups, width)
    tail = jnp.pad(tail, ((0, pad_rows - 3 * groups), (0, 0)))
    keyed_all = lax.all_gather(jnp.concatenate([keyed, tail], axis=0), "mp", axis=0)
    right_all = lax.all_gather(value_right, "mp", axis=0)
    left_all = lax.all_gather(key_left, "mp", axis=0)

    key_peer, value_peer = swap(key_weight), swap(value_weight)
    partial = forward(
        side_ref, keyed_all, key_weight, key_peer, value_weight, value_peer,
        key_right, value_left, right_all, model ** -0.5, hidden ** -0.5,
    )
    mixed = lax.psum_scatter(partial, "mp", scatter_dimension=0, tiled=False)
    mixed = jnp.swapaxes(mixed.reshape(2, members, width), 0, 1).reshape(2 * members, width)

    fitness = (2 * ranks - (population - 1)).astype(jnp.float32) / (population - 1)
    scaled_right = (fitness[:, None] * key_right.astype(jnp.float32)).astype(jnp.bfloat16)
    scaled_left = (fitness[:, None] * value_left.astype(jnp.float32)).astype(jnp.bfloat16)
    other = (1 - side) * half
    left_peer = swap(lax.dynamic_slice_in_dim(left_all, other, half, 0))
    right_peer = swap(lax.dynamic_slice_in_dim(right_all, other, half, 0))
    step = step_scale / population
    new_key = key_step(
        side_ref, left_all, left_peer, scaled_right, swap(scaled_right), key_weight, step
    )
    new_value = value_step(
        side_ref, scaled_left, swap(scaled_left), right_all, right_peer, value_weight, step
    )
    return (mixed, new_key, new_value)


def solution(mesh):
    placed = (
        P("grp", None),
        P(("grp", "pop")),
        P("pop", "mp"),
        P("mp"),
        P("pop", "mp"),
        P("mp", "pop"),
        P(("grp", "pop"), "mp"),
        P(("grp", "pop"), "mp"),
        P(("grp", "pop"), "mp"),
        P(("grp", "pop"), "mp"),
    )
    return jax.shard_map(
        shards,
        mesh=mesh,
        in_specs=placed,
        out_specs=(P(("grp", "pop"), "mp"), P(("grp", "pop"), "mp"), P(("grp", "mp"), "pop")),
        check_vma=False,
    )
```

time: 565 us -> 288 us (0.51)
  waiting for transfers between devices: 322 us -> 177 us
  local copies, waits for them, and re-layouts: 113 us -> 29.1 us
  matrix products: 79.8 us -> 0 us
  Pallas kernels: 0 us -> 59.8 us
  other arithmetic: 30.7 us -> 5.52 us
    reduce_scatter x4 -> x1, waiting for transfers between devices: 171 us -> 63.8 us  [shards(): mixed = lax.psum_scatter(partial, 'mp', scatter_dimension=0, tiled=False)]
    dot_general x6 -> x0, matrix products: 79.8 us -> none  [the longest x2 27.2 us: contract_first(): lax.dot_general(left, right, (((0,), (0,)), ((), ())), preferred_element_...]
    pallas_call x0 -> x3, Pallas kernels: none -> 59.8 us  [the longest x1 37.9 us: forward(): pl.pallas_call(functools.partial(forward_kernel, inv_model, inv_hidden),...]
    unnamed x16 -> x21, local copies, waits for them, and re-layouts: 53.9 us -> 3.99 us
    all_gather x5 -> x3, waiting for transfers between devices: 148 us -> 112 us  [the longest x1 76.3 us: shards(): lax.all_gather(jnp.concatenate([keyed, tail], axis=0), 'mp', axis=0)]
    convert_element_type x6, other arithmetic: 29.3 us -> 3.58 us  [the longest x1 3.34 us: shards(): (fitness[:, None] * value_left.astype(jnp.float32)).astype(jnp.bfloat16)]
    mul x5 -> x0, local copies, waits for them, and re-layouts: 17 us -> none  [the longest x3 10.4 us: shards(): noise_scale * inv_model * inner_key[:, :, None]]
    convert_element_type x1 -> x0, local copies, waits for them, and re-layouts: 10.9 us -> none  [shards(): spread = jnp.broadcast_to(right_full[:, None, :], (members, 2, count)).re...]
  transfers between devices with their start and end apart: 9 -> 11, of which waited for: 9 -> 4; matrix products, arithmetic and copies ran while one was open for 29% -> 10% of each run, Pallas kernels for 0% -> 21%
where the time goes in v1:
time: 288 us; the launch traced here: 287 us
  waiting for transfers between devices  177 us (61%)
  Pallas kernels  59.8 us (21%)
  local copies, waits for them, and re-layouts  29.1 us (10%)
  between operations  14 us (5%)
  other arithmetic  5.52 us (2%)
    all_gather x1, waiting for transfers between devices, shards(): lax.all_gather(jnp.concatenate([keyed, tail], axis=0), 'mp', axis=0)  76.3 us
    reduce_scatter x1, waiting for transfers between devices, shards(): mixed = lax.psum_scatter(partial, 'mp', scatter_dimension=0, tiled=False)  63.8 us
    pallas_call x1, Pallas kernels, forward(): pl.pallas_call(functools.partial(forward_kernel, inv_model, inv_hidden),...  37.9 us
    all_gather x1, waiting for transfers between devices, shards(): right_all = lax.all_gather(value_right, 'mp', axis=0)  29.8 us
    gather x2, local copies, waits for them, and re-layouts, look(): jnp.take(embedding, jnp.clip(ids, 0, half_vocab - 1), axis=0, mode='clip')  20.1 us
    pallas_call x1, Pallas kernels, value_step(): pl.pallas_call(functools.partial(value_step_kernel, step), out_shape=jax....  11.1 us
    pallas_call x1, Pallas kernels, key_step(): pl.pallas_call(functools.partial(key_step_kernel, step), out_shape=jax.Sh...  10.8 us
    all_gather x1, waiting for transfers between devices, shards(): left_all = lax.all_gather(key_left, 'mp', axis=0)  6.26 us
  transfers between devices with their start and end apart: 11, of which 4 were waited for; matrix products, arithmetic and copies ran while one was open for 10% of the time, Pallas kernels for 21%

profile of v1, /device:TPU:0, one launch (start us, length us, event | category | flops | bytes accessed | tf_op | source)
XLA Modules:
  0.0 287.4 jit_solution(11515885828223299793)
XLA Ops:
  7.2 0.7 all-gather.9.cloned.1.call-update
  7.9 0.7 clamp_bitcast_fusion
  8.7 9.9 %gather_fusion.1 = bf16[512,512]{1,0:T(8,128)(2,1)S(1)} fusion(bf16[16384,512]{1,0:T(8,128)(2,1)} %param.12, s32[1024]{0:T(1024)S(1)} %pad_clamp_fusion), kind=kCustom, calls=%fused_computation.1 | custom fusion | bytes 1050624 | tf_op jit(solution)/shard_map/jit(_take)/gather | solution.py:242
  18.6 0.5 collective-permute-start
  19.1 10.2 %gather_fusion = bf16[512,512]{1,0:T(8,128)(2,1)S(1)} fusion(bf16[16384,512]{1,0:T(8,128)(2,1)} %param.12, s32[1024]{0:T(1024)S(1)} %pad_clamp_fusion.1), kind=kCustom, calls=%fused_computation | custom fusion | bytes 1050624 | tf_op jit(solution)/shard_map/jit(_take)/gather | solution.py:242
  30.5 0.8 pad_maximum_fusion
  31.5 0.4 collective-permute-start.2
  32.3 29.8 %all-gather.9.cloned.1.call-done = bf16[2048,512]{1,0:T(8,128)(2,1)} async-done(((bf16[256,512]{1,0:T(8,128)(2,1)}), bf16[2048,512]{1,0:T(8,128)(2,1)}) %all-gather.9.cloned.1.call-update) | async-done | bytes 2097168 | tf_op jit(solution)/shard_map/all_gather | solution.py:264
  62.1 76.3 %all-gather.7.cloned.1.call-done = bf16[4224,512]{1,0:T(8,128)(2,1)} async-done(((bf16[528,512]{1,0:T(8,128)(2,1)}), bf16[4224,512]{1,0:T(8,128)(2,1)}) %all-gather.7.cloned.1.call-update) | async-done | bytes 4325392 | tf_op jit(solution)/shard_map/all_gather | solution.py:263
  138.4 37.9 %forward.1 = bf16[8,512,512]{2,1,0:T(8,128)(2,1)} custom-call(s32[1]{0:T(128)} %bitcast.side_ref, bf16[8,528,512]{2,1,0:T(8,128)(2,1)} %bitcast.37, bf16[2048,2048]{1,0:T(8,128)(2,1)} %weight.2, bf16[2048,2048]{1,0:T(8,128)(2,1)} %collective-permute-done.1.key_peer, bf16[2048,2048]{1,0:T(8,128)(2,1)} %weight.3, ...), custom_call_target="tpu_custom_call" | custom-call | flops 17179869184 | bytes 41943040 | tf_op jit(solution)/shard_map/forward/pallas_call | solution.py:106
  176.4 0.7 copy-done.8
  177.0 3.3 %multiply_convert_fusion = (bf16[256,2048]{1,0:T(8,128)(2,1)}, bf16[256,2048]{1,0:T(8,128)(2,1)S(1)}) fusion(bf16[256,2048]{1,0:T(8,128)(2,1)} %value_left.1, f32[256]{0:T(256)S(1)} %convert_multiply_fusion.1, bf16[256,2048]{1,0:T(8,128)(2,1)} %key_right.1), kind=kLoop, calls=%fused_computation.2 | loop fusion | flops 3145728 | bytes 4195328 | tf_op jit(solution)/shard_map/convert_element_type | solution.py:277
  180.4 1.1 constant_dynamic-slice_fusion
  181.5 0.4 collective-permute-start.6
  182.0 6.3 %all-gather.11.cloned.1.call-done = bf16[2048,512]{1,0:T(8,128)(2,1)} async-done(((bf16[256,512]{1,0:T(8,128)(2,1)}), bf16[2048,512]{1,0:T(8,128)(2,1)}) %all-gather.11.cloned.1.call-update) | async-done | bytes 2097168 | tf_op jit(solution)/shard_map/all_gather | solution.py:265
  188.3 1.3 constant_dynamic-slice_fusion.1
  189.7 1.0 copy-done.3
  190.7 11.1 %value_step.1 = bf16[2048,2048]{1,0:T(8,128)(2,1)} custom-call(s32[1]{0:T(128)} %bitcast.side_ref, bf16[256,2048]{1,0:T(8,128)(2,1)} %get-tuple-element.9.left_own, bf16[256,2048]{1,0:T(8,128)(2,1)} %collective-permute-done.5.left_peer, bf16[8,256,512]{2,1,0:T(8,128)(2,1)} %bitcast.24, bf16[4,256,512]{2,1,0:T(8,128)(2,1)} %copy-done.3, bf16[2048,2048]{1,0:T(8,128)(2,1)} %weight.3), custom_call_target="tpu_custom_call" | custom-call | flops 4294967296 | bytes 20971520 | tf_op jit(solution)/shard_map/value_step/pallas_call | solution.py:195
  201.7 1.0 copy-done.2
  202.7 1.0 copy-done.4
  203.7 10.8 %key_step.1 = bf16[2048,2048]{1,0:T(8,128)(2,1)} custom-call(s32[1]{0:T(128)} %bitcast.side_ref, bf16[8,256,512]{2,1,0:T(8,128)(2,1)} %bitcast.27, bf16[4,256,512]{2,1,0:T(8,128)(2,1)} %copy-done.4, bf16[256,2048]{1,0:T(8,128)(2,1)} %copy-done.1, bf16[256,2048]{1,0:T(8,128)(2,1)} %copy-done.2, bf16[2048,2048]{1,0:T(8,128)(2,1)} %weight.2), custom_call_target="tpu_custom_call" | custom-call | flops 4294967296 | bytes 20971520 | tf_op jit(solution)/shard_map/key_step/pallas_call | solution.py:154
  214.5 63.8 %reduce-scatter.2.cloned.1.call-done = bf16[1,512,512]{2,1,0:T(8,128)(2,1)} async-done(((bf16[8,512,512]{2,1,0:T(8,128)(2,1)}), bf16[1,512,512]{2,1,0:T(8,128)(2,1)}) %reduce-scatter.2.cloned.1.call-update) | async-done | bytes 524304 | tf_op jit(solution)/shard_map/reduce_scatter | solution.py:272
  278.3 1.6 copy.16
  279.9 1.0 reshape.138
  (48 shorter events, 1.9 us)
Async XLA Ops:
  7.2 55.0 %all-gather.9.cloned.1.call-start = ((), (), s32[]{:S(2)}) async-start(), calls=%async_computation.3 | async-start | bytes 2359296 | tf_op jit(solution)/shard_map/all_gather | solution.py:264
  7.9 130.5 %all-gather.7.cloned.1.call-start = ((), (), s32[]{:S(2)}) async-start(), calls=%async_computation.2 | async-start | bytes 4866048 | tf_op jit(solution)/shard_map/all_gather | solution.py:263
  18.6 10.9 %collective-permute-start = (bf16[512,512]{1,0:T(8,128)(2,1)S(1)}, bf16[512,512]{1,0:T(8,128)(2,1)S(1)}, u32[]{:S(2)}, u32[]{:S(2)}) collective-permute-start(bf16[512,512]{1,0:T(8,128)(2,1)S(1)} %gather_fusion.1), channel_id=1, source_target_pairs={{0,8},{8,0},{1,9},{9,1},{2,10},{10,2},{3,11},{11,3},{4,12},{12,4},... | collective-permute-start | bytes 1572872 | tf_op jit(solution)/shard_map/ppermute | solution.py:233
  19.1 10.2 %copy-start.6 = (s32[512,2]{0,1:T(2,128)S(1)}, s32[512,2]{0,1:T(2,128)}, u32[]{:S(2)}) copy-start(s32[512,2]{0,1:T(2,128)} %param.10) | copy-start | bytes 12292
  19.1 10.3 %copy-start.5 = (bf16[256,512]{1,0:T(8,128)(2,1)S(1)}, bf16[256,512]{1,0:T(8,128)(2,1)}, u32[]{:S(2)}) copy-start(bf16[256,512]{1,0:T(8,128)(2,1)} %param.16) | copy-start | bytes 786436
  29.4 0.7 copy-start.7
  31.3 156.9 %all-gather.11.cloned.1.call-start = ((), (), s32[]{:S(2)}) async-start(), calls=%async_computation.4 | async-start | bytes 2359296 | tf_op jit(solution)/shard_map/all_gather | solution.py:265
  31.4 107.0 %collective-permute-start.1 = (bf16[2048,2048]{1,0:T(8,128)(2,1)}, bf16[2048,2048]{1,0:T(8,128)(2,1)}, u32[]{:S(2)}, u32[]{:S(2)}) collective-permute-start(bf16[2048,2048]{1,0:T(8,128)(2,1)} %weight.2), channel_id=1, source_target_pairs={{0,8},{8,0},{1,9},{9,1},{2,10},{10,2},{3,11},{11,3},{4,12},{12,4},... | collective-permute-start | bytes 25165832 | tf_op jit(solution)/shard_map/ppermute | solution.py:233
  31.5 106.9 %collective-permute-start.2 = (bf16[2048,2048]{1,0:T(8,128)(2,1)}, bf16[2048,2048]{1,0:T(8,128)(2,1)}, u32[]{:S(2)}, u32[]{:S(2)}) collective-permute-start(bf16[2048,2048]{1,0:T(8,128)(2,1)} %weight.3), channel_id=1, source_target_pairs={{0,8},{8,0},{1,9},{9,1},{2,10},{10,2},{3,11},{11,3},{4,12},{12,4},... | collective-permute-start | bytes 25165832 | tf_op jit(solution)/shard_map/ppermute | solution.py:233
  32.1 246.3 %reduce-scatter.2.cloned.1.call-start = ((), (), s32[]{:S(2)}) async-start(), calls=%async_computation.1 | async-start | bytes 4718592 | tf_op jit(solution)/shard_map/reduce_scatter | solution.py:272
  176.3 0.7 copy-start.8
  177.0 3.3 %copy-start = (bf16[2048,512]{1,0:T(8,128)(2,1)S(1)}, bf16[2048,512]{1,0:T(8,128)(2,1)}, u32[]{:S(2)}) copy-start(bf16[2048,512]{1,0:T(8,128)(2,1)} %all-gather.9.cloned.1.call-done) | copy-start | bytes 6291460
  180.4 9.2 %copy-start.1 = (bf16[256,2048]{1,0:T(8,128)(2,1)}, bf16[256,2048]{1,0:T(8,128)(2,1)S(1)}, u32[]{:S(2)}) copy-start(bf16[256,2048]{1,0:T(8,128)(2,1)S(1)} %get-tuple-element.10.right_own) | copy-start | bytes 3145732
  180.4 9.3 %collective-permute-start.5 = (bf16[256,2048]{1,0:T(8,128)(2,1)}, bf16[256,2048]{1,0:T(8,128)(2,1)}, u32[]{:S(2)}, u32[]{:S(2)}) collective-permute-start(bf16[256,2048]{1,0:T(8,128)(2,1)} %get-tuple-element.9.left_own), channel_id=1, source_target_pairs={{0,8},{8,0},{1,9},{9,1},{2,10},{10,2},{3,11},{11,3},{4,12},{12,4},... | collective-permute-start | bytes 3145736 | tf_op jit(solution)/shard_map/ppermute | solution.py:233
  181.5 8.2 %collective-permute-start.6 = (bf16[4,256,512]{2,1,0:T(8,128)(2,1)}, bf16[4,256,512]{2,1,0:T(8,128)(2,1)S(1)}, u32[]{:S(2)}, u32[]{:S(2)}) collective-permute-start(bf16[4,256,512]{2,1,0:T(8,128)(2,1)} %constant_dynamic-slice_fusion), channel_id=1, source_target_pairs={{0,8},{8,0},{1,9},{9,1},{2,10},{10,2},{3,11},{11,3},{4,12},{12,4},... | collective-permute-start | bytes 3145736 | tf_op jit(solution)/shard_map/ppermute | solution.py:233
  181.9 19.8 %collective-permute-start.4 = (bf16[256,2048]{1,0:T(8,128)(2,1)S(1)}, bf16[256,2048]{1,0:T(8,128)(2,1)S(1)}, u32[]{:S(2)}, u32[]{:S(2)}) collective-permute-start(bf16[256,2048]{1,0:T(8,128)(2,1)S(1)} %get-tuple-element.10.right_own), channel_id=1, source_target_pairs={{0,8},{8,0},{1,9},{9,1},{2,10},{10,2},{3,11},{11,3},{4,12},{12,4},... | collective-permute-start | bytes 3145736 | tf_op jit(solution)/shard_map/ppermute | solution.py:233
  189.6 12.2 %collective-permute-start.3 = (bf16[4,256,512]{2,1,0:T(8,128)(2,1)S(1)}, bf16[4,256,512]{2,1,0:T(8,128)(2,1)S(1)}, u32[]{:S(2)}, u32[]{:S(2)}) collective-permute-start(bf16[4,256,512]{2,1,0:T(8,128)(2,1)S(1)} %constant_dynamic-slice_fusion.1), channel_id=1, source_target_pairs={{0,8},{8,0},{1,9},{9,1},{2,10},{10,2},{3,11},{11,3},{4,12},{12,4},... | collective-permute-start | bytes 3145736 | tf_op jit(solution)/shard_map/ppermute | solution.py:233
  189.7 1.0 copy-start.3
  201.7 1.0 copy-start.2
  202.7 1.0 copy-start.4
Sparse Core Ops, SparseCore 0:
  10.1 51.9 all-gather.8
  64.9 73.4 all-gather.6
  140.6 47.6 all-gather.10
  191.8 86.5 reduce-scatter.1

commit v2 on v1

--- a/solution.py
+++ b/solution.py
@@ -136,6 +136,361 @@
     )(side, keyed, key_own, key_peer, value_own, value_peer, key_right, value_left, value_right)
 
 
+def coordinates():
+    place = lax.axis_index("mp")
+    return lax.div(place, 2), lax.rem(place, 2)
+
+
+def pick(z, table):
+    total = 0
+    for value, row in enumerate(table):
+        total = total + (1 - lax.div(lax.rem(z + 4 - value, 4) + 3, 4)) * row
+    return total
+
+
+def greet(z, y):
+    barrier = pltpu.get_barrier_semaphore()
+
+    def tell(zz, yy):
+        pl.semaphore_signal(
+            barrier, inc=1, device_id={"mp": 2 * zz + yy}, device_id_type=pl.DeviceIdType.MESH
+        )
+
+    tell(z, 1 - y)
+    pl.when(z > 0)(lambda: tell(z - 1, y))
+    pl.when(z < 3)(lambda: tell(z + 1, y))
+    pl.semaphore_wait(barrier, 1 + lax.div(z + 3, 4) + lax.div(6 - z, 4))
+
+
+def remote(source, target, send, recv, zz, yy):
+    return pltpu.make_async_remote_copy(
+        src_ref=source,
+        dst_ref=target,
+        send_sem=send,
+        recv_sem=recv,
+        device_id={"mp": 2 * zz + yy},
+        device_id_type=pl.DeviceIdType.MESH,
+    )
+
+
+def split(row):
+    high = row.astype(jnp.bfloat16)
+    rest = row - high.astype(jnp.float32)
+    middle = rest.astype(jnp.bfloat16)
+    low = (rest - middle.astype(jnp.float32)).astype(jnp.bfloat16)
+    return high, middle, low
+
+
+def as_tail(row):
+    line = lax.broadcasted_iota(jnp.int32, row.shape, 0)
+    high, middle, low = [term.astype(jnp.float32) for term in split(row)]
+    kept = jnp.where(line == 0, high, jnp.where(line == 1, middle, jnp.where(line == 2, low, 0.0)))
+    return kept.astype(jnp.bfloat16)
+
+
+def from_tail(tail):
+    total = jnp.sum(tail.astype(jnp.float32), axis=0, keepdims=True)
+    return jnp.broadcast_to(total, tail.shape)
+
+
+gather_order = ((0, 1, 2, 3), (1, 0, 2, 3), (2, 3, 1, 0), (3, 2, 1, 0))
+scatter_order = ((3, 2, 1, 0), (3, 0, 2, 1), (0, 3, 1, 2), (0, 1, 2, 3))
+
+
+def gather_key_kernel(
+    inv_model, keyed, key_own, key_peer, key_right, value_left, squared, inner_value,
+    held, loaded, projected, inner_key, load_sem, right_sem, left_sem, across_sem, recv_sem,
+):
+    z, y = coordinates()
+    side = lax.axis_index("pop")
+    slices, padded, width = held.shape
+    tokens, half = padded - pad_rows, slices // 2
+    hidden = key_own.shape[1]
+    members = key_right.shape[0]
+    order = [pick(z, [row[k] for row in gather_order]) for k in range(4)]
+    own = [2 * b + y for b in order]
+    other = [2 * b + 1 - y for b in order]
+    sequence = [own[0], own[1], other[0], own[2], other[1], own[3], other[2], other[3]]
+
+    def load(k):
+        block, slot = sequence[k], k % 2
+        row = pl.multiple_of(lax.rem(block, half) * width, width)
+        from_own = lax.div(block, half) == side
+
+        @pl.when(from_own)
+        def _():
+            pltpu.make_async_copy(
+                key_own.at[pl.ds(row, width), :], loaded.at[slot], load_sem.at[slot]
+            ).start()
+
+        @pl.when(jnp.logical_not(from_own))
+        def _():
+            pltpu.make_async_copy(
+                key_peer.at[pl.ds(row, width), :], loaded.at[slot], load_sem.at[slot]
+            ).start()
+
+    load(0)
+    held[own[0]] = keyed[...]
+    greet(z, y)
+
+    def go_right(b):
+        block = held.at[2 * b + y]
+        return remote(block, block, right_sem.at[b], recv_sem.at[2 * b + y], z + 1, y)
+
+    def go_left(b):
+        block = held.at[2 * b + y]
+        return remote(block, block, left_sem.at[b], recv_sem.at[2 * b + y], z - 1, y)
+
+    def go_across(b):
+        block = held.at[2 * b + y]
+        return remote(block, block, across_sem.at[b], recv_sem.at[2 * b + y], z, 1 - y)
+
+    def arrived(block):
+        pltpu.make_async_copy(held.at[block], held.at[block], recv_sem.at[block]).wait()
+
+    def forward_on(k, act):
+        b = order[k]
+        pl.when((b <= z) & (z < 3))(lambda: act(go_right(b)))
+        pl.when((b >= z) & (z > 0))(lambda: act(go_left(b)))
+        act(go_across(b))
+
+    ones = jnp.ones((pad_rows, 128), jnp.bfloat16)
+    chunk = 512
+
+    def compute(k):
+        block, slot = sequence[k], k % 2
+        if k + 1 < len(sequence):
+            load(k + 1)
+        pltpu.make_async_copy(
+            key_own.at[pl.ds(0, width), :], loaded.at[slot], load_sem.at[slot]
+        ).wait()
+        partial = contract_first(held[block, tokens:, :], ones)
+        inner_key[...] = partial if k == 0 else inner_key[...] + partial
+
+        @pl.loop(0, hidden // chunk)
+        def _(c):
+            cols = pl.ds(pl.multiple_of(c * chunk, chunk), chunk)
+            product = dot(held[block, :tokens, :], loaded[slot, :, cols])
+            projected[:, cols] = product if k == 0 else projected[:, cols] + product
+
+    k = 0
+    for step in range(4):
+        if step > 0:
+            arrived(own[step])
+        forward_on(step, lambda copy: copy.start())
+        compute(k)
+        k += 1
+        if step > 0:
+            arrived(other[step - 1])
+            compute(k)
+            k += 1
+    arrived(other[3])
+    compute(k)
+
+    factor = inner_key[...] * (noise_scale * inv_model)
+    inner_key[...] = factor
+    inner_value[...] = jnp.zeros_like(inner_value)
+
+    @pl.loop(0, hidden // 128)
+    def _(c):
+        cols = pl.ds(pl.multiple_of(c * 128, 128), 128)
+        right = key_right[:, cols].astype(jnp.float32)
+        left = value_left[:, cols].astype(jnp.float32)
+        for t in range(tokens // members):
+            rows = slice(t * members, (t + 1) * members)
+            value = projected[rows, cols] * inv_model + inner_key[rows, :] * right
+            rounded = (jnp.maximum(value, 0.0) ** 2).astype(jnp.bfloat16)
+            squared[rows, cols] = rounded
+            inner_value[rows, :] += rounded.astype(jnp.float32) * left
+
+    for step in range(4):
+        forward_on(step, lambda copy: copy.wait_send())
+
+
+def gather_key(keyed, key_own, key_peer, key_right, value_left, inv_model):
+    padded, width = keyed.shape
+    tokens = padded - pad_rows
+    hidden = key_own.shape[1]
+    slices = 8
+    vmem = pl.BlockSpec(memory_space=pltpu.VMEM)
+    hbm = pl.BlockSpec(memory_space=pl.ANY)
+    return pl.pallas_call(
+        functools.partial(gather_key_kernel, inv_model),
+        out_shape=(
+            jax.ShapeDtypeStruct((tokens, hidden), jnp.bfloat16),
+            jax.ShapeDtypeStruct((tokens, 128), jnp.float32),
+        ),
+        in_specs=[vmem, hbm, hbm, vmem, vmem],
+        out_specs=(vmem, vmem),
+        scratch_shapes=[
+            pltpu.VMEM((slices, padded, width), jnp.bfloat16),
+            pltpu.VMEM((2, width, hidden), jnp.bfloat16),
+            pltpu.VMEM((tokens, hidden), jnp.float32),
+            pltpu.VMEM((tokens, 128), jnp.float32),
+            pltpu.SemaphoreType.DMA((2,)),
+            pltpu.SemaphoreType.DMA((4,)),
+            pltpu.SemaphoreType.DMA((4,)),
+            pltpu.SemaphoreType.DMA((4,)),
+            pltpu.SemaphoreType.DMA((slices,)),
+        ],
+        compiler_params=pltpu.CompilerParams(
+            vmem_limit_bytes=vmem_bytes, collective_id=1, has_side_effects=True
+        ),
+        cost_estimate=pl.CostEstimate(
+            flops=16 * tokens * width * hidden,
+            bytes_accessed=16 * width * hidden,
+            transcendentals=0,
+        ),
+        name="gather_key",
+    )(keyed, key_own, key_peer, key_right, value_left)
+
+
+def value_scatter_kernel(
+    inv_hidden, squared, inner_value, value_own, value_peer, value_right, out,
+    loaded, total, inner, across, from_across, to_right, to_left, from_left, from_right,
+    load_sem, across_sem, across_recv, right_sem, left_sem, left_recv, right_recv,
+):
+    z, y = coordinates()
+    side = lax.axis_index("pop")
+    rows, width = loaded.shape[1], loaded.shape[2]
+    tokens = squared.shape[0]
+    members = value_right.shape[0]
+    half = 4
+    order = [pick(z, [row[k] for row in scatter_order]) for k in range(4)]
+    sequence = []
+    for t in order:
+        sequence += [2 * t + 1 - y, 2 * t + y]
+
+    def load(k):
+        block, slot = sequence[k], k % 2
+        column = pl.multiple_of(lax.rem(block, half) * width, width)
+        from_own = lax.div(block, half) == side
+
+        @pl.when(from_own)
+        def _():
+            pltpu.make_async_copy(
+                value_own.at[:, pl.ds(column, width)], loaded.at[slot], load_sem.at[slot]
+            ).start()
+
+        @pl.when(jnp.logical_not(from_own))
+        def _():
+            pltpu.make_async_copy(
+                value_peer.at[:, pl.ds(column, width)], loaded.at[slot], load_sem.at[slot]
+            ).start()
+
+    load(0)
+    greet(z, y)
+    ones = jnp.ones((pad_rows, 128), jnp.bfloat16)
+    row = jnp.zeros((pad_rows, tokens), jnp.float32)
+    for term in split(inner_value[...]):
+        row += lax.dot_general(
+            ones, term, (((1,), (1,)), ((), ())), preferred_element_type=jnp.float32
+        )
+
+    def go_across(t):
+        return remote(
+            across.at[t], from_across.at[t], across_sem.at[t], across_recv.at[t], z, 1 - y
+        )
+
+    def go_right(t):
+        return remote(
+            to_right.at[t], from_left.at[t], right_sem.at[t], left_recv.at[t], z + 1, y
+        )
+
+    def go_left(t):
+        return remote(
+            to_left.at[t], from_right.at[t], left_sem.at[t], right_recv.at[t], z - 1, y
+        )
+
+    chunk = 256
+    for k in range(8):
+        slot, t = k % 2, order[k // 2]
+        if k + 1 < 8:
+            load(k + 1)
+        pltpu.make_async_copy(
+            value_own.at[:, pl.ds(0, width)], loaded.at[slot], load_sem.at[slot]
+        ).wait()
+
+        @pl.loop(0, width // chunk)
+        def _(c):
+            cols = pl.ds(pl.multiple_of(c * chunk, chunk), chunk)
+            product = dot(squared[...], loaded[slot, :, cols])
+            if k % 2 == 0:
+                across[t, :tokens, cols] = product.astype(jnp.bfloat16)
+            else:
+                total[t, :, cols] = product
+
+        if k % 2 == 0:
+            across[t, tokens:, :] = as_tail(row)
+            go_across(t).start()
+
+    def take(t, arrivals, recv):
+        pltpu.make_async_copy(arrivals.at[t], arrivals.at[t], recv.at[t]).wait()
+        total[t] += arrivals[t, :tokens, :].astype(jnp.float32)
+        inner[t] += from_tail(arrivals[t, tokens:, :])
+
+    def put(t, departures, copy):
+        departures[t, :tokens, :] = total[t].astype(jnp.bfloat16)
+        departures[t, tokens:, :] = as_tail(inner[t])
+        copy.start()
+
+    for t in order:
+        inner[t] = row
+        take(t, from_across, across_recv)
+        pl.when((t >= z) & (z > 0))(lambda: take(t, from_left, left_recv))
+        pl.when((t <= z) & (z < 3))(lambda: take(t, from_right, right_recv))
+        pl.when(t > z)(lambda: put(t, to_right, go_right(t)))
+        pl.when(t < z)(lambda: put(t, to_left, go_left(t)))
+
+    amount = contract_first(as_tail(inner[z]), ones) * noise_scale
+    for t in range(tokens // members):
+        own = slice(t * members, (t + 1) * members)
+        for c in range(0, width, 128):
+            cols = slice(c, c + 128)
+            spread = value_right[:, cols].astype(jnp.float32)
+            out[own, cols] = (
+                (total[z, own, cols] + amount[own, :] * spread) * inv_hidden
+            ).astype(jnp.bfloat16)
+
+    for t in order:
+        go_across(t).wait_send()
+        pl.when(t > z)(lambda: go_right(t).wait_send())
+        pl.when(t < z)(lambda: go_left(t).wait_send())
+
+
+def value_scatter(squared, inner_value, value_own, value_peer, value_right, inv_hidden):
+    tokens = squared.shape[0]
+    rows = value_own.shape[0]
+    width = value_right.shape[1]
+    vmem = pl.BlockSpec(memory_space=pltpu.VMEM)
+    hbm = pl.BlockSpec(memory_space=pl.ANY)
+    message = pltpu.VMEM((4, tokens + pad_rows, width), jnp.bfloat16)
+    sems = pltpu.SemaphoreType.DMA((4,))
+    return pl.pallas_call(
+        functools.partial(value_scatter_kernel, inv_hidden),
+        out_shape=jax.ShapeDtypeStruct((tokens, width), jnp.bfloat16),
+        in_specs=[vmem, vmem, hbm, hbm, vmem],
+        out_specs=vmem,
+        scratch_shapes=[
+            pltpu.VMEM((2, rows, width), jnp.bfloat16),
+            pltpu.VMEM((4, tokens, width), jnp.float32),
+            pltpu.VMEM((4, pad_rows, tokens), jnp.float32),
+            message, message, message, message, message, message,
+            pltpu.SemaphoreType.DMA((2,)),
+            sems, sems, sems, sems, sems, sems,
+        ],
+        compiler_params=pltpu.CompilerParams(
+            vmem_limit_bytes=vmem_bytes, collective_id=2, has_side_effects=True
+        ),
+        cost_estimate=pl.CostEstimate(
+            flops=16 * tokens * width * rows,
+            bytes_accessed=16 * width * rows,
+            transcendentals=0,
+        ),
+        name="value_scatter",
+    )(squared, inner_value, value_own, value_peer, value_right)
+
+
 def key_step_kernel(step, side_ref, left_own, left_peer, right_own, right_peer, weight, out_ref):
     columns = out_ref.shape[1]
     chunk = min(512, columns)
@@ -253,23 +608,27 @@
     inner = jnp.sum(
         keyed.astype(jnp.float32).reshape(2, members, width) * left[None], axis=2
     ).reshape(-1)
-    high = inner.astype(jnp.bfloat16)
-    rest = inner - high.astype(jnp.float32)
-    middle = rest.astype(jnp.bfloat16)
-    low = (rest - middle.astype(jnp.float32)).astype(jnp.bfloat16)
     groups = -(-2 * members // width)
-    tail = jnp.stack([high, middle, low]).reshape(3 * groups, width)
+    tail = jnp.stack(split(inner)).reshape(3 * groups, width)
     tail = jnp.pad(tail, ((0, pad_rows - 3 * groups), (0, 0)))
-    keyed_all = lax.all_gather(jnp.concatenate([keyed, tail], axis=0), "mp", axis=0)
+    keyed = jnp.concatenate([keyed, tail], axis=0)
     right_all = lax.all_gather(value_right, "mp", axis=0)
     left_all = lax.all_gather(key_left, "mp", axis=0)
 
     key_peer, value_peer = swap(key_weight), swap(value_weight)
-    partial = forward(
-        side_ref, keyed_all, key_weight, key_peer, value_weight, value_peer,
-        key_right, value_left, right_all, model ** -0.5, hidden ** -0.5,
-    )
-    mixed = lax.psum_scatter(partial, "mp", scatter_dimension=0, tiled=False)
+    if slices == 8 and 2 * members == width:
+        squared, inner_value = gather_key(
+            keyed, key_weight, key_peer, key_right, value_left, model ** -0.5
+        )
+        mixed = value_scatter(
+            squared, inner_value, value_weight, value_peer, value_right, hidden ** -0.5
+        )
+    else:
+        partial = forward(
+            side_ref, lax.all_gather(keyed, "mp", axis=0), key_weight, key_peer, value_weight,
+            value_peer, key_right, value_left, right_all, model ** -0.5, hidden ** -0.5,
+        )
+        mixed = lax.psum_scatter(partial, "mp", scatter_dimension=0, tiled=False)
     mixed = jnp.swapaxes(mixed.reshape(2, members, width), 0, 1).reshape(2 * members, width)
 
     fitness = (2 * ranks - (population - 1)).astype(jnp.float32) / (population - 1)

time: 288 us -> 266 us (0.924)
  waiting for transfers between devices: 177 us -> 73.7 us
  Pallas kernels: 59.8 us -> 139 us
    pallas_call x1 -> x2, Pallas kernels: 37.9 us -> 117 us  [the longest x1 63.4 us: gather_key(): pl.pallas_call(functools.partial(gather_key_kernel, inv_model), out_shape...]
    all_gather x1 -> x0, waiting for transfers between devices: 76.3 us -> none  [shards(): lax.all_gather(jnp.concatenate([keyed, tail], axis=0), 'mp', axis=0)]
    reduce_scatter x1 -> x0, waiting for transfers between devices: 63.8 us -> none  [shards(): mixed = lax.psum_scatter(partial, 'mp', scatter_dimension=0, tiled=False)]
    all_gather x1, waiting for transfers between devices: 6.26 us -> 25.7 us  [shards(): left_all = lax.all_gather(key_left, 'mp', axis=0)]
    all_gather x1, waiting for transfers between devices: 29.8 us -> 46.8 us  [shards(): right_all = lax.all_gather(value_right, 'mp', axis=0)]
    unnamed x21, local copies, waits for them, and re-layouts: 3.99 us -> 1.04 us
  transfers between devices with their start and end apart: 11 -> 9, of which waited for: 4 -> 3; matrix products, arithmetic and copies ran while one was open for 10% -> 12% of each run, Pallas kernels for 21% -> 32%
where the time goes in v2:
time: 266 us; the launch traced here: 265 us
  Pallas kernels  139 us (52%)
  waiting for transfers between devices  73.7 us (28%)
  local copies, waits for them, and re-layouts  28.5 us (11%)
  between operations  14.2 us (5%)
  other arithmetic  7.89 us (3%)
    pallas_call x1, Pallas kernels, gather_key(): pl.pallas_call(functools.partial(gather_key_kernel, inv_model), out_shape...  63.4 us
    pallas_call x1, Pallas kernels, value_scatter(): pl.pallas_call(functools.partial(value_scatter_kernel, inv_hidden), out_s...  53.6 us
    all_gather x1, waiting for transfers between devices, shards(): right_all = lax.all_gather(value_right, 'mp', axis=0)  46.8 us
    all_gather x1, waiting for transfers between devices, shards(): left_all = lax.all_gather(key_left, 'mp', axis=0)  25.7 us
    gather x2, local copies, waits for them, and re-layouts, look(): jnp.take(embedding, jnp.clip(ids, 0, half_vocab - 1), axis=0, mode='clip')  21.3 us
    pallas_call x1, Pallas kernels, value_step(): pl.pallas_call(functools.partial(value_step_kernel, step), out_shape=jax....  11 us
    pallas_call x1, Pallas kernels, key_step(): pl.pallas_call(functools.partial(key_step_kernel, step), out_shape=jax.Sh...  10.7 us
  transfers between devices with their start and end apart: 9, of which 3 were waited for; matrix products, arithmetic and copies ran while one was open for 12% of the time, Pallas kernels for 32%

profile of v2, /device:TPU:0, one launch (start us, length us, event | category | flops | bytes accessed | tf_op | source)
XLA Modules:
  0.0 264.9 jit_solution(9088250750566490582)
XLA Ops:
  7.2 0.7 all-gather.5.cloned.1.call-update
  7.9 0.5 collective-permute-start.1
  8.7 0.7 clamp_bitcast_fusion
  9.4 10.7 %gather_fusion.1 = bf16[512,512]{1,0:T(8,128)(2,1)} fusion(bf16[16384,512]{1,0:T(8,128)(2,1)} %param.12, s32[1024]{0:T(1024)S(1)} %pad_clamp_fusion), kind=kCustom, calls=%fused_computation.1 | custom fusion | bytes 1050624 | tf_op jit(solution)/shard_map/jit(_take)/gather | solution.py:597
  20.1 0.5 collective-permute-start
  20.5 1.9 multiply_convert_fusion
  22.6 0.5 collective-permute-start.5
  23.1 0.9 convert_element_type.113
  24.0 10.6 %gather_fusion = bf16[512,512]{1,0:T(8,128)(2,1)} fusion(bf16[16384,512]{1,0:T(8,128)(2,1)} %param.12, s32[1024]{0:T(1024)S(1)} %pad_clamp_fusion.1), kind=kCustom, calls=%fused_computation | custom fusion | bytes 1050624 | tf_op jit(solution)/shard_map/jit(_take)/gather | solution.py:597
  35.1 1.3 select_convert_fusion
  36.4 25.7 %all-gather.5.cloned.1.call-done = bf16[2048,512]{1,0:T(8,128)(2,1)} async-done(((bf16[256,512]{1,0:T(8,128)(2,1)}), bf16[2048,512]{1,0:T(8,128)(2,1)}) %all-gather.5.cloned.1.call-update) | async-done | bytes 2097168 | tf_op jit(solution)/shard_map/all_gather | solution.py:616
  62.1 2.3 constant_dynamic-slice_fusion.1
  64.4 0.8 multiply_add_fusion.1
  65.3 46.8 %all-gather.7.cloned.1.call-done = bf16[2048,512]{1,0:T(8,128)(2,1)} async-done(((bf16[256,512]{1,0:T(8,128)(2,1)}), bf16[2048,512]{1,0:T(8,128)(2,1)}) %all-gather.7.cloned.1.call-update) | async-done | bytes 2097168 | tf_op jit(solution)/shard_map/all_gather | solution.py:615
  112.1 1.3 constant_dynamic-slice_fusion
  113.5 1.2 fusion
  114.8 0.8 pad_maximum_fusion.keyed
  115.7 10.7 %key_step.1 = bf16[2048,2048]{1,0:T(8,128)(2,1)} custom-call(s32[1]{0:T(128)} %bitcast.7.side_ref, bf16[8,256,512]{2,1,0:T(8,128)(2,1)} %bitcast.23, bf16[4,256,512]{2,1,0:T(8,128)(2,1)} %collective-permute-done.3.left_peer, bf16[256,2048]{1,0:T(8,128)(2,1)} %copy-done.1, bf16[256,2048]{1,0:T(8,128)(2,1)} %collective-permute-done.4.right_peer, ...), custom_call_target="tpu_custom_call" | custom-call | flops 4294967296 | bytes 20971520 | tf_op jit(solution)/shard_map/key_step/pallas_call | solution.py:509
  126.4 1.0 copy-done.3
  127.4 11.0 %value_step.1 = bf16[2048,2048]{1,0:T(8,128)(2,1)} custom-call(s32[1]{0:T(128)} %bitcast.7.side_ref, bf16[256,2048]{1,0:T(8,128)(2,1)} %copy-done, bf16[256,2048]{1,0:T(8,128)(2,1)} %collective-permute-done.5.left_peer, bf16[8,256,512]{2,1,0:T(8,128)(2,1)} %bitcast.25, bf16[4,256,512]{2,1,0:T(8,128)(2,1)} %copy-done.3, bf16[2048,2048]{1,0:T(8,128)(2,1)} %weight.3), custom_call_target="tpu_custom_call" | custom-call | flops 4294967296 | bytes 20971520 | tf_op jit(solution)/shard_map/value_step/pallas_call | solution.py:550
  138.4 63.4 %gather_key.1 = (bf16[512,2048]{1,0:T(8,128)(2,1)}, f32[512,128]{1,0:T(8,128)}) custom-call(bf16[528,512]{1,0:T(8,128)(2,1)} %pad_maximum_fusion.keyed, bf16[2048,2048]{1,0:T(8,128)(2,1)} %weight.2, bf16[2048,2048]{1,0:T(8,128)(2,1)} %collective-permute-done.1.key_peer, bf16[256,2048]{1,0:T(8,128)(2,1)} %key_right.1, bf16[256,2048]{1,0:T(8,128)(2,1)} %value_left.1), custom_call_target="tpu_custom_call" | custom-call | flops 8589934592 | bytes 16777216 | tf_op jit(solution)/shard_map/gather_key/pallas_call | solution.py:317
  201.8 53.6 %value_scatter.1 = bf16[512,512]{1,0:T(8,128)(2,1)} custom-call(bf16[512,2048]{1,0:T(8,128)(2,1)} %get-tuple-element.5.squared, f32[512,128]{1,0:T(8,128)} %get-tuple-element.6.inner_value, bf16[2048,2048]{1,0:T(8,128)(2,1)} %weight.3, bf16[2048,2048]{1,0:T(8,128)(2,1)} %collective-permute-done.2.value_peer, bf16[256,512]{1,0:T(8,128)(2,1)} %value_right.1), custom_call_target="tpu_custom_call" | custom-call | flops 8589934592 | bytes 16777216 | tf_op jit(solution)/shard_map/value_scatter/pallas_call | solution.py:469
  255.5 1.6 copy.16
  257.0 1.0 reshape.141
  (43 shorter events, 1.0 us)
Async XLA Ops:
  7.2 55.0 %all-gather.5.cloned.1.call-start = ((), (), s32[]{:S(2)}) async-start(), calls=%async_computation | async-start | bytes 2359296 | tf_op jit(solution)/shard_map/all_gather | solution.py:616
  7.9 104.2 %all-gather.7.cloned.1.call-start = ((), (), s32[]{:S(2)}) async-start(), calls=%async_computation.1 | async-start | bytes 2359296 | tf_op jit(solution)/shard_map/all_gather | solution.py:615
  7.9 130.5 %collective-permute-start.1 = (bf16[2048,2048]{1,0:T(8,128)(2,1)}, bf16[2048,2048]{1,0:T(8,128)(2,1)}, u32[]{:S(2)}, u32[]{:S(2)}) collective-permute-start(bf16[2048,2048]{1,0:T(8,128)(2,1)} %weight.2), channel_id=1, source_target_pairs={{0,8},{8,0},{1,9},{9,1},{2,10},{10,2},{3,11},{11,3},{4,12},{12,4},... | collective-permute-start | bytes 25165832 | tf_op jit(solution)/shard_map/ppermute | solution.py:588
  8.5 193.4 %collective-permute-start.2 = (bf16[2048,2048]{1,0:T(8,128)(2,1)}, bf16[2048,2048]{1,0:T(8,128)(2,1)}, u32[]{:S(2)}, u32[]{:S(2)}) collective-permute-start(bf16[2048,2048]{1,0:T(8,128)(2,1)} %weight.3), channel_id=1, source_target_pairs={{0,8},{8,0},{1,9},{9,1},{2,10},{10,2},{3,11},{11,3},{4,12},{12,4},... | collective-permute-start | bytes 25165832 | tf_op jit(solution)/shard_map/ppermute | solution.py:588
  9.4 11.1 %copy-start.8 = (s32[256]{0:T(256)S(1)}, s32[256]{0:T(256)}, u32[]{:S(2)}) copy-start(s32[256]{0:T(256)} %param.11) | copy-start | bytes 3076
  9.4 11.1 %copy-start.2 = (bf16[256,2048]{1,0:T(8,128)(2,1)S(1)}, bf16[256,2048]{1,0:T(8,128)(2,1)}, u32[]{:S(2)}) copy-start(bf16[256,2048]{1,0:T(8,128)(2,1)} %key_right.1) | copy-start | bytes 3145732
  20.1 15.0 %collective-permute-start = (bf16[512,512]{1,0:T(8,128)(2,1)}, bf16[512,512]{1,0:T(8,128)(2,1)}, u32[]{:S(2)}, u32[]{:S(2)}) collective-permute-start(bf16[512,512]{1,0:T(8,128)(2,1)} %gather_fusion.1), channel_id=1, source_target_pairs={{0,8},{8,0},{1,9},{9,1},{2,10},{10,2},{3,11},{11,3},{4,12},{12,4},... | collective-permute-start | bytes 1572872 | tf_op jit(solution)/shard_map/ppermute | solution.py:588
  20.5 2.6 copy-start.4
  22.5 12.1 %copy-start = (bf16[256,2048]{1,0:T(8,128)(2,1)}, bf16[256,2048]{1,0:T(8,128)(2,1)S(1)}, u32[]{:S(2)}) copy-start(bf16[256,2048]{1,0:T(8,128)(2,1)S(1)} %get-tuple-element.13.left_own) | copy-start | bytes 3145732
  22.5 12.1 %copy-start.1 = (bf16[256,2048]{1,0:T(8,128)(2,1)}, bf16[256,2048]{1,0:T(8,128)(2,1)S(1)}, u32[]{:S(2)}) copy-start(bf16[256,2048]{1,0:T(8,128)(2,1)S(1)} %get-tuple-element.14.right_own) | copy-start | bytes 3145732
  22.5 90.9 %collective-permute-start.4 = (bf16[256,2048]{1,0:T(8,128)(2,1)S(1)}, bf16[256,2048]{1,0:T(8,128)(2,1)}, u32[]{:S(2)}, u32[]{:S(2)}) collective-permute-start(bf16[256,2048]{1,0:T(8,128)(2,1)S(1)} %get-tuple-element.14.right_own), channel_id=1, source_target_pairs={{0,8},{8,0},{1,9},{9,1},{2,10},{10,2},{3,11},{11,3},{4,12},{12,4},... | collective-permute-start | bytes 3145736 | tf_op jit(solution)/shard_map/ppermute | solution.py:588
  22.6 103.7 %collective-permute-start.5 = (bf16[256,2048]{1,0:T(8,128)(2,1)S(1)}, bf16[256,2048]{1,0:T(8,128)(2,1)}, u32[]{:S(2)}, u32[]{:S(2)}) collective-permute-start(bf16[256,2048]{1,0:T(8,128)(2,1)S(1)} %get-tuple-element.13.left_own), channel_id=1, source_target_pairs={{0,8},{8,0},{1,9},{9,1},{2,10},{10,2},{3,11},{11,3},{4,12},{12,4},... | collective-permute-start | bytes 3145736 | tf_op jit(solution)/shard_map/ppermute | solution.py:588
  24.0 10.6 %copy-start.6 = (s32[512,2]{0,1:T(2,128)S(1)}, s32[512,2]{0,1:T(2,128)}, u32[]{:S(2)}) copy-start(s32[512,2]{0,1:T(2,128)} %param.10) | copy-start | bytes 12292
  34.7 29.7 %copy-start.7 = (f32[512]{0:T(512)S(1)}, f32[512]{0:T(512)}, u32[]{:S(2)}) copy-start(f32[512]{0:T(512)} %param.13) | copy-start | bytes 6148
  64.4 51.2 %collective-permute-start.3 = (bf16[4,256,512]{2,1,0:T(8,128)(2,1)}, bf16[4,256,512]{2,1,0:T(8,128)(2,1)}, u32[]{:S(2)}, u32[]{:S(2)}) collective-permute-start(bf16[4,256,512]{2,1,0:T(8,128)(2,1)} %constant_dynamic-slice_fusion.1), channel_id=1, source_target_pairs={{0,8},{8,0},{1,9},{9,1},{2,10},{10,2},{3,11},{11,3},{4,12},{12,4},... | collective-permute-start | bytes 3145736 | tf_op jit(solution)/shard_map/ppermute | solution.py:588
  65.3 48.2 %copy-start.5 = (bf16[256,512]{1,0:T(8,128)(2,1)S(1)}, bf16[256,512]{1,0:T(8,128)(2,1)}, u32[]{:S(2)}) copy-start(bf16[256,512]{1,0:T(8,128)(2,1)} %get-tuple-element.8) | copy-start | bytes 786436
  113.4 13.0 %collective-permute-start.6 = (bf16[4,256,512]{2,1,0:T(8,128)(2,1)S(1)}, bf16[4,256,512]{2,1,0:T(8,128)(2,1)S(1)}, u32[]{:S(2)}, u32[]{:S(2)}) collective-permute-start(bf16[4,256,512]{2,1,0:T(8,128)(2,1)S(1)} %constant_dynamic-slice_fusion), channel_id=1, source_target_pairs={{0,8},{8,0},{1,9},{9,1},{2,10},{10,2},{3,11},{11,3},{4,12},{12,4},... | collective-permute-start | bytes 3145736 | tf_op jit(solution)/shard_map/ppermute | solution.py:588
  126.4 1.0 copy-start.3
Sparse Core Ops, SparseCore 0:
  10.1 51.9 all-gather.4
  64.3 47.7 all-gather.6

commit v3 on v2

--- a/solution.py
+++ b/solution.py
@@ -491,7 +491,9 @@
     )(squared, inner_value, value_own, value_peer, value_right)
 
 
-def key_step_kernel(step, side_ref, left_own, left_peer, right_own, right_peer, weight, out_ref):
+def key_step_kernel(
+    step, side_ref, left_own, left_peer, right_own, right_peer, weight, after, out_ref
+):
     columns = out_ref.shape[1]
     chunk = min(512, columns)
     own, peer = left_own[0], left_peer[0]
@@ -501,7 +503,7 @@
         out_ref[:, cols] = (weight[:, cols].astype(jnp.float32) + step * grad).astype(jnp.bfloat16)
 
 
-def key_step(side, left_all, left_peer, right_own, right_peer, weight, step):
+def key_step(side, left_all, left_peer, right_own, right_peer, weight, step, after):
     half, members, width = left_peer.shape
     rows, columns = weight.shape
     fixed = pl.BlockSpec((members, columns), lambda j, s: (0, 0))
@@ -518,6 +520,7 @@
                 fixed,
                 fixed,
                 tile,
+                pl.BlockSpec(memory_space=pl.ANY),
             ],
             out_specs=tile,
         ),
@@ -528,10 +531,12 @@
             transcendentals=0,
         ),
         name="key_step",
-    )(side, left_all, left_peer, right_own, right_peer, weight)
-
-
-def value_step_kernel(step, side_ref, left_own, left_peer, right_all, right_peer, weight, out_ref):
+    )(side, left_all, left_peer, right_own, right_peer, weight, after)
+
+
+def value_step_kernel(
+    step, side_ref, left_own, left_peer, right_all, right_peer, weight, after, out_ref
+):
     half, _, width = right_peer.shape
     mine = side_ref[0] * half
     own, peer = left_own[...], left_peer[...]
@@ -541,7 +546,7 @@
         out_ref[:, cols] = (weight[:, cols].astype(jnp.float32) + step * grad).astype(jnp.bfloat16)
 
 
-def value_step(side, left_own, left_peer, right_all, right_peer, weight, step):
+def value_step(side, left_own, left_peer, right_all, right_peer, weight, step, after):
     half, members, width = right_peer.shape
     rows, columns = weight.shape
     size = min(512, rows)
@@ -559,6 +564,7 @@
                 pl.BlockSpec(right_all.shape, lambda i, s: (0, 0, 0)),
                 pl.BlockSpec(right_peer.shape, lambda i, s: (0, 0, 0)),
                 tile,
+                pl.BlockSpec(memory_space=pl.ANY),
             ],
             out_specs=tile,
         ),
@@ -569,7 +575,7 @@
             transcendentals=0,
         ),
         name="value_step",
-    )(side, left_own, left_peer, right_all, right_peer, weight)
+    )(side, left_own, left_peer, right_all, right_peer, weight, after)
 
 
 def shards(
@@ -590,16 +596,18 @@
     half_vocab = embedding.shape[0]
     by_side = jnp.swapaxes(token_ids.reshape(2, members, 2), 1, 2)
 
-    def look(which):
-        ids = lax.dynamic_index_in_dim(by_side, which, 0, keepdims=False).reshape(-1)
-        ids = ids - side * half_vocab
-        inside = (ids >= 0) & (ids < half_vocab)
-        return jnp.take(embedding, jnp.clip(ids, 0, half_vocab - 1), axis=0, mode="clip"), inside
-
-    theirs, _ = look(1 - side)
-    received = swap(theirs)
-    mine, inside = look(side)
-    rows = jnp.where(inside[:, None], mine, received).astype(jnp.float32)
+    tokens = 2 * members
+    ids = jnp.concatenate(
+        [
+            lax.dynamic_index_in_dim(by_side, side, 0, keepdims=False).reshape(-1),
+            lax.dynamic_index_in_dim(by_side, 1 - side, 0, keepdims=False).reshape(-1),
+        ]
+    )
+    ids = ids - side * half_vocab
+    inside = (ids[:tokens] >= 0) & (ids[:tokens] < half_vocab)
+    looked = jnp.take(embedding, jnp.clip(ids, 0, half_vocab - 1), axis=0, mode="clip")
+    received = swap(looked[tokens:])
+    rows = jnp.where(inside[:, None], looked[:tokens], received).astype(jnp.float32)
     first, second = rows[:members], rows[members:]
     keyed = jnp.concatenate(
         [first + (0.0 - first) * mix_key, second + (first - second) * mix_key], axis=0
@@ -620,15 +628,18 @@
         squared, inner_value = gather_key(
             keyed, key_weight, key_peer, key_right, value_left, model ** -0.5
         )
+        right_all, squared = lax.optimization_barrier((right_all, squared))
         mixed = value_scatter(
             squared, inner_value, value_weight, value_peer, value_right, hidden ** -0.5
         )
+        left_all, mixed = lax.optimization_barrier((left_all, mixed))
     else:
         partial = forward(
             side_ref, lax.all_gather(keyed, "mp", axis=0), key_weight, key_peer, value_weight,
             value_peer, key_right, value_left, right_all, model ** -0.5, hidden ** -0.5,
         )
         mixed = lax.psum_scatter(partial, "mp", scatter_dimension=0, tiled=False)
+    summed = mixed
     mixed = jnp.swapaxes(mixed.reshape(2, members, width), 0, 1).reshape(2 * members, width)
 
     fitness = (2 * ranks - (population - 1)).astype(jnp.float32) / (population - 1)
@@ -639,10 +650,12 @@
     right_peer = swap(lax.dynamic_slice_in_dim(right_all, other, half, 0))
     step = step_scale / population
     new_key = key_step(
-        side_ref, left_all, left_peer, scaled_right, swap(scaled_right), key_weight, step
+        side_ref, left_all, left_peer, scaled_right, swap(scaled_right), key_weight, step,
+        summed,
     )
     new_value = value_step(
-        side_ref, scaled_left, swap(scaled_left), right_all, right_peer, value_weight, step
+        side_ref, scaled_left, swap(scaled_left), right_all, right_peer, value_weight, step,
+        summed,
     )
     return (mixed, new_key, new_value)
 

time: 266 us -> 227 us (0.85)
  waiting for transfers between devices: 73.7 us -> 8.78 us
  Pallas kernels: 139 us -> 176 us
  local copies, waits for them, and re-layouts: 28.5 us -> 19.6 us
    all_gather x1, waiting for transfers between devices: 46.8 us -> 0.02 us  [shards(): right_all = lax.all_gather(value_right, 'mp', axis=0)]
    pallas_call x1, Pallas kernels: 63.4 us -> 97.1 us  [gather_key(): pl.pallas_call(functools.partial(gather_key_kernel, inv_model), out_shape...]
    all_gather x1, waiting for transfers between devices: 25.7 us -> 0.02 us  [shards(): left_all = lax.all_gather(key_left, 'mp', axis=0)]
    gather x2 -> x1, local copies, waits for them, and re-layouts: 21.3 us -> 11.9 us  [shards(): jnp.take(embedding, jnp.clip(ids, 0, half_vocab - 1), axis=0, mode='clip')]
    ppermute x7, waiting for transfers between devices: 0.42 us -> 8.64 us  [shards(): swap = lambda array: lax.ppermute(array, 'pop', [(0, 1), (1, 0)])]
    pallas_call x1, Pallas kernels: 53.6 us -> 56.9 us  [value_scatter(): pl.pallas_call(functools.partial(value_scatter_kernel, inv_hidden), out_s...]
  transfers between devices with their start and end apart: 9 -> 9, of which waited for: 3 -> 1; matrix products, arithmetic and copies ran while one was open for 12% -> 11% of each run, Pallas kernels for 32% -> 73%
where the time goes in v3:
time: 227 us; the launch traced here: 226 us
  Pallas kernels  176 us (78%)
  local copies, waits for them, and re-layouts  19.6 us (9%)
  between operations  14.3 us (6%)
  waiting for transfers between devices  8.78 us (4%)
  other arithmetic  5.57 us (2%)
    pallas_call x1, Pallas kernels, gather_key(): pl.pallas_call(functools.partial(gather_key_kernel, inv_model), out_shape...  97.1 us
    pallas_call x1, Pallas kernels, value_scatter(): pl.pallas_call(functools.partial(value_scatter_kernel, inv_hidden), out_s...  56.9 us
    gather x1, local copies, waits for them, and re-layouts, shards(): jnp.take(embedding, jnp.clip(ids, 0, half_vocab - 1), axis=0, mode='clip')  11.9 us
    pallas_call x1, Pallas kernels, value_step(): pl.pallas_call(functools.partial(value_step_kernel, step), out_shape=jax....  11.1 us
    pallas_call x1, Pallas kernels, key_step(): pl.pallas_call(functools.partial(key_step_kernel, step), out_shape=jax.Sh...  10.7 us
    ppermute x7, waiting for transfers between devices, shards(): swap = lambda array: lax.ppermute(array, 'pop', [(0, 1), (1, 0)])  8.64 us
  transfers between devices with their start and end apart: 9, of which 1 were waited for; matrix products, arithmetic and copies ran while one was open for 11% of the time, Pallas kernels for 73%

profile of v3, /device:TPU:0, one launch (start us, length us, event | category | flops | bytes accessed | tf_op | source)
XLA Modules:
  0.0 225.8 jit_solution(4885201499545186732)
XLA Ops:
  7.2 0.5 collective-permute-start.1
  7.7 0.1 collective-permute-start.2
  7.8 0.1 all-gather.7.cloned.1.call-update
  7.9 0.7 reshape.129
  8.7 11.9 %gather_fusion = bf16[1024,512]{1,0:T(8,128)(2,1)S(1)} fusion(bf16[16384,512]{1,0:T(8,128)(2,1)} %param.12, s32[1024]{0:T(1024)S(1)} %broadcast_clamp_fusion), kind=kCustom, calls=%fused_computation | custom fusion | bytes 2101248 | tf_op jit(solution)/shard_map/jit(_take)/gather | solution.py:608
  20.6 0.8 slice.24
  21.5 0.5 collective-permute-start
  22.0 2.2 multiply_convert_fusion
  24.2 0.1 collective-permute-start.5
  24.4 0.5 collective-permute-start.4
  24.8 0.9 convert_element_type.113
  25.7 8.6 %collective-permute-done = bf16[512,512]{1,0:T(8,128)(2,1)} collective-permute-done((bf16[512,512]{1,0:T(8,128)(2,1)}, bf16[512,512]{1,0:T(8,128)(2,1)}, u32[]{:S(2)}, u32[]{:S(2)}) %collective-permute-start) | collective-permute-done | bytes 524320 | tf_op jit(solution)/shard_map/ppermute | solution.py:594
  34.4 1.2 fusion.1
  35.6 0.1 multiply_add_fusion.1
  35.8 0.2 fusion
  36.0 0.8 pad_maximum_fusion.keyed
  36.9 97.1 %gather_key.1 = (bf16[512,2048]{1,0:T(8,128)(2,1)}, f32[512,128]{1,0:T(8,128)}) custom-call(bf16[528,512]{1,0:T(8,128)(2,1)} %pad_maximum_fusion.keyed, bf16[2048,2048]{1,0:T(8,128)(2,1)} %weight.2, bf16[2048,2048]{1,0:T(8,128)(2,1)} %collective-permute-done.1.key_peer, bf16[256,2048]{1,0:T(8,128)(2,1)} %key_right.1, bf16[256,2048]{1,0:T(8,128)(2,1)} %value_left.1), custom_call_target="tpu_custom_call" | custom-call | flops 8589934592 | bytes 16777216 | tf_op jit(solution)/shard_map/gather_key/pallas_call | solution.py:317
  134.0 2.3 %constant_dynamic-slice_fusion = bf16[4,256,512]{2,1,0:T(8,128)(2,1)} fusion(bf16[8,256,512]{2,1,0:T(8,128)(2,1)} %bitcast.24, s32[]{:T(128)S(6)} %select_n.18), kind=kLoop, calls=%fused_computation.25 | loop fusion | bytes 2097156 | tf_op jit(solution)/shard_map/dynamic_slice | solution.py:650
  136.3 56.9 %value_scatter.1.after = bf16[512,512]{1,0:T(8,128)(2,1)} custom-call(bf16[512,2048]{1,0:T(8,128)(2,1)} %get-tuple-element.10.squared, f32[512,128]{1,0:T(8,128)} %get-tuple-element.11.inner_value, bf16[2048,2048]{1,0:T(8,128)(2,1)} %weight.3, bf16[2048,2048]{1,0:T(8,128)(2,1)} %collective-permute-done.2.value_peer, bf16[256,512]{1,0:T(8,128)(2,1)} %value_right.1), custom_call_target="tpu_custom_call" | custom-call | flops 8589934592 | bytes 16777216 | tf_op jit(solution)/shard_map/value_scatter/pallas_call | solution.py:469
  193.2 2.3 %constant_dynamic-slice_fusion.1 = bf16[4,256,512]{2,1,0:T(8,128)(2,1)} fusion(bf16[8,256,512]{2,1,0:T(8,128)(2,1)} %bitcast.26, s32[]{:T(128)S(6)} %select_n.18), kind=kLoop, calls=%fused_computation.26 | loop fusion | bytes 2097156 | tf_op jit(solution)/shard_map/dynamic_slice | solution.py:649
  195.5 0.5 copy.13
  196.1 1.0 reshape.133
  197.1 11.1 %value_step.1 = bf16[2048,2048]{1,0:T(8,128)(2,1)} custom-call(s32[1]{0:T(128)} %bitcast.12.side_ref, bf16[256,2048]{1,0:T(8,128)(2,1)} %copy-done.2, bf16[256,2048]{1,0:T(8,128)(2,1)} %collective-permute-done.5.left_peer, bf16[8,256,512]{2,1,0:T(8,128)(2,1)} %bitcast.25, bf16[4,256,512]{2,1,0:T(8,128)(2,1)} %collective-permute-done.6.right_peer, ...), custom_call_target="tpu_custom_call" | custom-call | flops 4294967296 | bytes 20971520 | tf_op jit(solution)/shard_map/value_step/pallas_call | solution.py:555
  208.2 10.7 %key_step.1 = bf16[2048,2048]{1,0:T(8,128)(2,1)} custom-call(s32[1]{0:T(128)} %bitcast.12.side_ref, bf16[8,256,512]{2,1,0:T(8,128)(2,1)} %bitcast.27, bf16[4,256,512]{2,1,0:T(8,128)(2,1)} %collective-permute-done.3.left_peer, bf16[256,2048]{1,0:T(8,128)(2,1)} %copy-done.1, bf16[256,2048]{1,0:T(8,128)(2,1)} %collective-permute-done.4.right_peer, ...), custom_call_target="tpu_custom_call" | custom-call | flops 4294967296 | bytes 20971520 | tf_op jit(solution)/shard_map/key_step/pallas_call | solution.py:511
  (38 shorter events, 0.3 us)
Async XLA Ops:
  7.2 126.8 %all-gather.7.cloned.1.call-start = ((), (), s32[]{:S(2)}) async-start(), calls=%async_computation.1 | async-start | bytes 2359296 | tf_op jit(solution)/shard_map/all_gather | solution.py:623
  7.2 29.7 %collective-permute-start.1 = (bf16[2048,2048]{1,0:T(8,128)(2,1)}, bf16[2048,2048]{1,0:T(8,128)(2,1)}, u32[]{:S(2)}, u32[]{:S(2)}) collective-permute-start(bf16[2048,2048]{1,0:T(8,128)(2,1)} %weight.2), channel_id=1, source_target_pairs={{0,8},{8,0},{1,9},{9,1},{2,10},{10,2},{3,11},{11,3},{4,12},{12,4},... | collective-permute-start | bytes 25165832 | tf_op jit(solution)/shard_map/ppermute | solution.py:594
  7.7 128.5 %collective-permute-start.2 = (bf16[2048,2048]{1,0:T(8,128)(2,1)}, bf16[2048,2048]{1,0:T(8,128)(2,1)}, u32[]{:S(2)}, u32[]{:S(2)}) collective-permute-start(bf16[2048,2048]{1,0:T(8,128)(2,1)} %weight.3), channel_id=1, source_target_pairs={{0,8},{8,0},{1,9},{9,1},{2,10},{10,2},{3,11},{11,3},{4,12},{12,4},... | collective-permute-start | bytes 25165832 | tf_op jit(solution)/shard_map/ppermute | solution.py:594
  7.9 185.3 %all-gather.5.cloned.1.call-start = ((), (), s32[]{:S(2)}) async-start(), calls=%async_computation | async-start | bytes 2359296 | tf_op jit(solution)/shard_map/all_gather | solution.py:624
  8.7 13.2 %copy-start.6 = (s32[256]{0:T(256)S(1)}, s32[256]{0:T(256)}, u32[]{:S(2)}) copy-start(s32[256]{0:T(256)} %param.11) | copy-start | bytes 3076
  21.5 12.9 %collective-permute-start = (bf16[512,512]{1,0:T(8,128)(2,1)}, bf16[512,512]{1,0:T(8,128)(2,1)}, u32[]{:S(2)}, u32[]{:S(2)}) collective-permute-start(bf16[512,512]{1,0:T(8,128)(2,1)} %slice.24), channel_id=1, source_target_pairs={{0,8},{8,0},{1,9},{9,1},{2,10},{10,2},{3,11},{11,3},{4,12},{12,4},... | collective-permute-start | bytes 1572872 | tf_op jit(solution)/shard_map/ppermute | solution.py:594
  22.0 2.9 %copy-start.4 = (bf16[256,512]{1,0:T(8,128)(2,1)S(1)}, bf16[256,512]{1,0:T(8,128)(2,1)}, u32[]{:S(2)}) copy-start(bf16[256,512]{1,0:T(8,128)(2,1)} %param.16) | copy-start | bytes 786436
  24.2 11.5 %copy-start.1 = (bf16[256,2048]{1,0:T(8,128)(2,1)}, bf16[256,2048]{1,0:T(8,128)(2,1)S(1)}, u32[]{:S(2)}) copy-start(bf16[256,2048]{1,0:T(8,128)(2,1)S(1)} %get-tuple-element.22.right_own) | copy-start | bytes 3145732
  24.2 11.5 %copy-start.2 = (bf16[256,2048]{1,0:T(8,128)(2,1)}, bf16[256,2048]{1,0:T(8,128)(2,1)S(1)}, u32[]{:S(2)}) copy-start(bf16[256,2048]{1,0:T(8,128)(2,1)S(1)} %get-tuple-element.21.left_own) | copy-start | bytes 3145732
  24.2 11.3 %copy-start.5 = (f32[512]{0:T(512)S(1)}, f32[512]{0:T(512)}, u32[]{:S(2)}) copy-start(f32[512]{0:T(512)} %param.13) | copy-start | bytes 6148
  24.2 172.8 %collective-permute-start.5 = (bf16[256,2048]{1,0:T(8,128)(2,1)S(1)}, bf16[256,2048]{1,0:T(8,128)(2,1)}, u32[]{:S(2)}, u32[]{:S(2)}) collective-permute-start(bf16[256,2048]{1,0:T(8,128)(2,1)S(1)} %get-tuple-element.21.left_own), channel_id=1, source_target_pairs={{0,8},{8,0},{1,9},{9,1},{2,10},{10,2},{3,11},{11,3},{4,12},{12,4},... | collective-permute-start | bytes 3145736 | tf_op jit(solution)/shard_map/ppermute | solution.py:594
  24.4 183.8 %collective-permute-start.4 = (bf16[256,2048]{1,0:T(8,128)(2,1)S(1)}, bf16[256,2048]{1,0:T(8,128)(2,1)}, u32[]{:S(2)}, u32[]{:S(2)}) collective-permute-start(bf16[256,2048]{1,0:T(8,128)(2,1)S(1)} %get-tuple-element.22.right_own), channel_id=1, source_target_pairs={{0,8},{8,0},{1,9},{9,1},{2,10},{10,2},{3,11},{11,3},{4,12},{12,4},... | collective-permute-start | bytes 3145736 | tf_op jit(solution)/shard_map/ppermute | solution.py:594
  25.7 10.1 %copy-start.3 = (f32[256,512]{1,0:T(8,128)S(1)}, f32[256,512]{1,0:T(8,128)}, u32[]{:S(2)}) copy-start(f32[256,512]{1,0:T(8,128)} %convert_element_type.113) | copy-start | bytes 1572868
  136.3 60.8 %collective-permute-start.6 = (bf16[4,256,512]{2,1,0:T(8,128)(2,1)}, bf16[4,256,512]{2,1,0:T(8,128)(2,1)}, u32[]{:S(2)}, u32[]{:S(2)}) collective-permute-start(bf16[4,256,512]{2,1,0:T(8,128)(2,1)} %constant_dynamic-slice_fusion), channel_id=1, source_target_pairs={{0,8},{8,0},{1,9},{9,1},{2,10},{10,2},{3,11},{11,3},{4,12},{12,4},... | collective-permute-start | bytes 3145736 | tf_op jit(solution)/shard_map/ppermute | solution.py:594
  193.2 2.4 %copy-start = (bf16[512,512]{1,0:T(8,128)(2,1)S(1)}, bf16[512,512]{1,0:T(8,128)(2,1)}, u32[]{:S(2)}) copy-start(bf16[512,512]{1,0:T(8,128)(2,1)} %value_scatter.1.after) | copy-start | bytes 1572868
  195.5 12.7 %collective-permute-start.3 = (bf16[4,256,512]{2,1,0:T(8,128)(2,1)}, bf16[4,256,512]{2,1,0:T(8,128)(2,1)}, u32[]{:S(2)}, u32[]{:S(2)}) collective-permute-start(bf16[4,256,512]{2,1,0:T(8,128)(2,1)} %constant_dynamic-slice_fusion.1), channel_id=1, source_target_pairs={{0,8},{8,0},{1,9},{9,1},{2,10},{10,2},{3,11},{11,3},{4,12},{12,4},... | collective-permute-start | bytes 3145736 | tf_op jit(solution)/shard_map/ppermute | solution.py:594
Sparse Core Ops, SparseCore 0:
  10.1 62.7 all-gather.6
  75.1 59.4 all-gather.4

commit v4 on v3

--- a/solution.py
+++ b/solution.py
@@ -621,19 +621,19 @@
     tail = jnp.pad(tail, ((0, pad_rows - 3 * groups), (0, 0)))
     keyed = jnp.concatenate([keyed, tail], axis=0)
     right_all = lax.all_gather(value_right, "mp", axis=0)
-    left_all = lax.all_gather(key_left, "mp", axis=0)
-
     key_peer, value_peer = swap(key_weight), swap(value_weight)
     if slices == 8 and 2 * members == width:
         squared, inner_value = gather_key(
             keyed, key_weight, key_peer, key_right, value_left, model ** -0.5
         )
-        right_all, squared = lax.optimization_barrier((right_all, squared))
+        right_all, later_left, squared = lax.optimization_barrier((right_all, key_left, squared))
+        left_all = lax.all_gather(later_left, "mp", axis=0)
         mixed = value_scatter(
             squared, inner_value, value_weight, value_peer, value_right, hidden ** -0.5
         )
         left_all, mixed = lax.optimization_barrier((left_all, mixed))
     else:
+        left_all = lax.all_gather(key_left, "mp", axis=0)
         partial = forward(
             side_ref, lax.all_gather(keyed, "mp", axis=0), key_weight, key_peer, value_weight,
             value_peer, key_right, value_left, right_all, model ** -0.5, hidden ** -0.5,

time: 227 us -> 230 us (1.013)
  waiting for transfers between devices: 8.78 us -> 12.1 us
    pallas_call x1, Pallas kernels: 56.9 us -> 77 us  [value_scatter(): pl.pallas_call(functools.partial(value_scatter_kernel, inv_hidden), out_s...]
    pallas_call x1, Pallas kernels: 97.1 us -> 79.3 us  [gather_key(): pl.pallas_call(functools.partial(gather_key_kernel, inv_model), out_shape...]
    ppermute x7, waiting for transfers between devices: 8.64 us -> 11.9 us  [shards(): swap = lambda array: lax.ppermute(array, 'pop', [(0, 1), (1, 0)])]
  transfers between devices with their start and end apart: 9 -> 9, of which waited for: 1 -> 1; matrix products, arithmetic and copies ran while one was open for 11% -> 10% of each run, Pallas kernels for 73% -> 73%
where the time goes in v4:
time: 230 us
  Pallas kernels  178 us (77%)
  local copies, waits for them, and re-layouts  18.6 us (8%)
  between operations  14.3 us (6%)
  waiting for transfers between devices  12.1 us (5%)
  other arithmetic  4.83 us (2%)
    pallas_call x1, Pallas kernels, gather_key(): pl.pallas_call(functools.partial(gather_key_kernel, inv_model), out_shape...  79.3 us
    pallas_call x1, Pallas kernels, value_scatter(): pl.pallas_call(functools.partial(value_scatter_kernel, inv_hidden), out_s...  77 us
    gather x1, local copies, waits for them, and re-layouts, shards(): jnp.take(embedding, jnp.clip(ids, 0, half_vocab - 1), axis=0, mode='clip')  12 us
    ppermute x7, waiting for transfers between devices, shards(): swap = lambda array: lax.ppermute(array, 'pop', [(0, 1), (1, 0)])  11.9 us
    pallas_call x1, Pallas kernels, value_step(): pl.pallas_call(functools.partial(value_step_kernel, step), out_shape=jax....  11 us
    pallas_call x1, Pallas kernels, key_step(): pl.pallas_call(functools.partial(key_step_kernel, step), out_shape=jax.Sh...  10.7 us
  transfers between devices with their start and end apart: 9, of which 1 were waited for; matrix products, arithmetic and copies ran while one was open for 10% of the time, Pallas kernels for 73%

profile of v4, /device:TPU:0, one launch (start us, length us, event | category | flops | bytes accessed | tf_op | source)
XLA Modules:
  0.0 229.5 jit_solution(5606695771875899406)
XLA Ops:
  7.2 0.5 collective-permute-start.1
  7.7 0.1 collective-permute-start.2
  7.8 0.1 all-gather.5.cloned.1.call-update
  7.9 0.0 all-gather.7.cloned.1.call-start
  7.9 0.7 reshape.129
  8.7 12.0 %gather_fusion = bf16[1024,512]{1,0:T(8,128)(2,1)S(1)} fusion(bf16[16384,512]{1,0:T(8,128)(2,1)} %param.12, s32[1024]{0:T(1024)S(1)} %broadcast_clamp_fusion), kind=kCustom, calls=%fused_computation | custom fusion | bytes 2101248 | tf_op jit(solution)/shard_map/jit(_take)/gather | solution.py:608
  20.7 0.5 collective-permute-start
  21.3 0.1 convert_element_type.113
  21.3 11.9 %collective-permute-done = bf16[512,512]{1,0:T(8,128)(2,1)S(1)} collective-permute-done((bf16[512,512]{1,0:T(8,128)(2,1)S(1)}, bf16[512,512]{1,0:T(8,128)(2,1)S(1)}, u32[]{:S(2)}, u32[]{:S(2)}) %collective-permute-start) | collective-permute-done | bytes 524320 | tf_op jit(solution)/shard_map/ppermute | solution.py:594
  33.3 0.1 fusion.1
  33.4 0.1 multiply_add_fusion.1
  33.6 0.2 fusion
  33.9 0.8 pad_maximum_fusion.keyed
  34.7 79.3 %gather_key.1 = (bf16[512,2048]{1,0:T(8,128)(2,1)}, f32[512,128]{1,0:T(8,128)}) custom-call(bf16[528,512]{1,0:T(8,128)(2,1)} %pad_maximum_fusion.keyed, bf16[2048,2048]{1,0:T(8,128)(2,1)} %weight.2, bf16[2048,2048]{1,0:T(8,128)(2,1)} %collective-permute-done.1.key_peer, bf16[256,2048]{1,0:T(8,128)(2,1)} %key_right.1, bf16[256,2048]{1,0:T(8,128)(2,1)} %value_left.1), custom_call_target="tpu_custom_call" | custom-call | flops 8589934592 | bytes 16777216 | tf_op jit(solution)/shard_map/gather_key/pallas_call | solution.py:317
  114.1 3.4 %multiply_convert_fusion = (bf16[256,2048]{1,0:T(8,128)(2,1)}, bf16[256,2048]{1,0:T(8,128)(2,1)S(1)}) fusion(bf16[256,2048]{1,0:T(8,128)(2,1)} %value_left.1, f32[256]{0:T(256)S(1)} %convert_multiply_fusion.1, bf16[256,2048]{1,0:T(8,128)(2,1)} %key_right.1), kind=kLoop, calls=%fused_computation.1 | loop fusion | flops 3145728 | bytes 4195328 | tf_op jit(solution)/shard_map/convert_element_type | solution.py:647
  117.4 0.5 collective-permute-start.4
  117.9 1.0 constant_dynamic-slice_fusion
  119.0 77.0 %value_scatter.1.after = bf16[512,512]{1,0:T(8,128)(2,1)} custom-call(bf16[512,2048]{1,0:T(8,128)(2,1)} %get-tuple-element.12.squared, f32[512,128]{1,0:T(8,128)} %get-tuple-element.13.inner_value, bf16[2048,2048]{1,0:T(8,128)(2,1)} %weight.3, bf16[2048,2048]{1,0:T(8,128)(2,1)} %collective-permute-done.2.value_peer, bf16[256,512]{1,0:T(8,128)(2,1)} %value_right.1), custom_call_target="tpu_custom_call" | custom-call | flops 8589934592 | bytes 16777216 | tf_op jit(solution)/shard_map/value_scatter/pallas_call | solution.py:469
  196.1 2.3 %constant_dynamic-slice_fusion.1 = bf16[4,256,512]{2,1,0:T(8,128)(2,1)} fusion(bf16[8,256,512]{2,1,0:T(8,128)(2,1)} %bitcast.26, s32[]{:T(128)S(6)} %select_n.18), kind=kLoop, calls=%fused_computation.26 | loop fusion | bytes 2097156 | tf_op jit(solution)/shard_map/dynamic_slice | solution.py:649
  198.4 0.5 copy.13
  199.0 1.0 reshape.133
  200.0 1.0 copy-done.3
  200.9 11.0 %value_step.1 = bf16[2048,2048]{1,0:T(8,128)(2,1)} custom-call(s32[1]{0:T(128)} %bitcast.12.side_ref, bf16[256,2048]{1,0:T(8,128)(2,1)} %get-tuple-element.23.left_own, bf16[256,2048]{1,0:T(8,128)(2,1)} %collective-permute-done.5.left_peer, bf16[8,256,512]{2,1,0:T(8,128)(2,1)} %bitcast.24, bf16[4,256,512]{2,1,0:T(8,128)(2,1)} %copy-done.3, ...), custom_call_target="tpu_custom_call" | custom-call | flops 4294967296 | bytes 20971520 | tf_op jit(solution)/shard_map/value_step/pallas_call | solution.py:555
  212.0 10.7 %key_step.1 = bf16[2048,2048]{1,0:T(8,128)(2,1)} custom-call(s32[1]{0:T(128)} %bitcast.12.side_ref, bf16[8,256,512]{2,1,0:T(8,128)(2,1)} %bitcast.27, bf16[4,256,512]{2,1,0:T(8,128)(2,1)} %collective-permute-done.3.left_peer, bf16[256,2048]{1,0:T(8,128)(2,1)} %copy-done.2, bf16[256,2048]{1,0:T(8,128)(2,1)} %collective-permute-done.4.right_peer, ...), custom_call_target="tpu_custom_call" | custom-call | flops 4294967296 | bytes 20971520 | tf_op jit(solution)/shard_map/key_step/pallas_call | solution.py:511
  (38 shorter events, 0.3 us)
Async XLA Ops:
  7.2 106.8 %all-gather.5.cloned.1.call-start = ((), (), s32[]{:S(2)}) async-start(), calls=%async_computation | async-start | bytes 2359296 | tf_op jit(solution)/shard_map/all_gather | solution.py:623
  7.2 27.5 %collective-permute-start.1 = (bf16[2048,2048]{1,0:T(8,128)(2,1)}, bf16[2048,2048]{1,0:T(8,128)(2,1)}, u32[]{:S(2)}, u32[]{:S(2)}) collective-permute-start(bf16[2048,2048]{1,0:T(8,128)(2,1)} %weight.2), channel_id=1, source_target_pairs={{0,8},{8,0},{1,9},{9,1},{2,10},{10,2},{3,11},{11,3},{4,12},{12,4},... | collective-permute-start | bytes 25165832 | tf_op jit(solution)/shard_map/ppermute | solution.py:594
  7.7 111.3 %collective-permute-start.2 = (bf16[2048,2048]{1,0:T(8,128)(2,1)}, bf16[2048,2048]{1,0:T(8,128)(2,1)}, u32[]{:S(2)}, u32[]{:S(2)}) collective-permute-start(bf16[2048,2048]{1,0:T(8,128)(2,1)} %weight.3), channel_id=1, source_target_pairs={{0,8},{8,0},{1,9},{9,1},{2,10},{10,2},{3,11},{11,3},{4,12},{12,4},... | collective-permute-start | bytes 25165832 | tf_op jit(solution)/shard_map/ppermute | solution.py:594
  7.9 188.2 %all-gather.7.cloned.1.call-start = ((), (), s32[]{:S(2)}) async-start(), calls=%async_computation.1 | async-start | bytes 2359296 | tf_op jit(solution)/shard_map/all_gather | solution.py:630
  8.7 12.6 %copy-start.4 = (bf16[256,512]{1,0:T(8,128)(2,1)S(1)}, bf16[256,512]{1,0:T(8,128)(2,1)}, u32[]{:S(2)}) copy-start(bf16[256,512]{1,0:T(8,128)(2,1)} %param.16) | copy-start | bytes 786436
  20.7 12.7 %copy-start.5 = (f32[512]{0:T(512)S(1)}, f32[512]{0:T(512)}, u32[]{:S(2)}) copy-start(f32[512]{0:T(512)} %param.13) | copy-start | bytes 6148
  20.7 12.5 %collective-permute-start = (bf16[512,512]{1,0:T(8,128)(2,1)S(1)}, bf16[512,512]{1,0:T(8,128)(2,1)S(1)}, u32[]{:S(2)}, u32[]{:S(2)}) collective-permute-start(bf16[512,512]{1,0:T(8,128)(2,1)S(1)} %slice.24), channel_id=1, source_target_pairs={{0,8},{8,0},{1,9},{9,1},{2,10},{10,2},{3,11},{11,3},{4,12},{12,4},... | collective-permute-start | bytes 1572872 | tf_op jit(solution)/shard_map/ppermute | solution.py:594
  34.7 79.3 %copy-start.6 = (s32[256]{0:T(256)S(1)}, s32[256]{0:T(256)}, u32[]{:S(2)}) copy-start(s32[256]{0:T(256)} %param.11) | copy-start | bytes 3076
  114.1 3.9 %copy-start = (bf16[2048,512]{1,0:T(8,128)(2,1)S(1)}, bf16[2048,512]{1,0:T(8,128)(2,1)}, u32[]{:S(2)}) copy-start(bf16[2048,512]{1,0:T(8,128)(2,1)} %all-gather.5.cloned.1.call-done) | copy-start | bytes 6291460
  117.4 78.6 %copy-start.2 = (bf16[256,2048]{1,0:T(8,128)(2,1)}, bf16[256,2048]{1,0:T(8,128)(2,1)S(1)}, u32[]{:S(2)}) copy-start(bf16[256,2048]{1,0:T(8,128)(2,1)S(1)} %get-tuple-element.24.right_own) | copy-start | bytes 3145732
  117.4 82.5 %collective-permute-start.5 = (bf16[256,2048]{1,0:T(8,128)(2,1)}, bf16[256,2048]{1,0:T(8,128)(2,1)}, u32[]{:S(2)}, u32[]{:S(2)}) collective-permute-start(bf16[256,2048]{1,0:T(8,128)(2,1)} %get-tuple-element.23.left_own), channel_id=1, source_target_pairs={{0,8},{8,0},{1,9},{9,1},{2,10},{10,2},{3,11},{11,3},{4,12},{12,4},... | collective-permute-start | bytes 3145736 | tf_op jit(solution)/shard_map/ppermute | solution.py:594
  117.4 94.5 %collective-permute-start.4 = (bf16[256,2048]{1,0:T(8,128)(2,1)S(1)}, bf16[256,2048]{1,0:T(8,128)(2,1)}, u32[]{:S(2)}, u32[]{:S(2)}) collective-permute-start(bf16[256,2048]{1,0:T(8,128)(2,1)S(1)} %get-tuple-element.24.right_own), channel_id=1, source_target_pairs={{0,8},{8,0},{1,9},{9,1},{2,10},{10,2},{3,11},{11,3},{4,12},{12,4},... | collective-permute-start | bytes 3145736 | tf_op jit(solution)/shard_map/ppermute | solution.py:594
  119.0 81.0 %collective-permute-start.6 = (bf16[4,256,512]{2,1,0:T(8,128)(2,1)}, bf16[4,256,512]{2,1,0:T(8,128)(2,1)S(1)}, u32[]{:S(2)}, u32[]{:S(2)}) collective-permute-start(bf16[4,256,512]{2,1,0:T(8,128)(2,1)} %constant_dynamic-slice_fusion), channel_id=1, source_target_pairs={{0,8},{8,0},{1,9},{9,1},{2,10},{10,2},{3,11},{11,3},{4,12},{12,4},... | collective-permute-start | bytes 3145736 | tf_op jit(solution)/shard_map/ppermute | solution.py:594
  196.1 2.4 %copy-start.1 = (bf16[512,512]{1,0:T(8,128)(2,1)S(1)}, bf16[512,512]{1,0:T(8,128)(2,1)}, u32[]{:S(2)}) copy-start(bf16[512,512]{1,0:T(8,128)(2,1)} %value_scatter.1.after) | copy-start | bytes 1572868
  198.4 13.6 %collective-permute-start.3 = (bf16[4,256,512]{2,1,0:T(8,128)(2,1)}, bf16[4,256,512]{2,1,0:T(8,128)(2,1)}, u32[]{:S(2)}, u32[]{:S(2)}) collective-permute-start(bf16[4,256,512]{2,1,0:T(8,128)(2,1)} %constant_dynamic-slice_fusion.1), channel_id=1, source_target_pairs={{0,8},{8,0},{1,9},{9,1},{2,10},{10,2},{3,11},{11,3},{4,12},{12,4},... | collective-permute-start | bytes 3145736 | tf_op jit(solution)/shard_map/ppermute | solution.py:594
  200.0 1.0 copy-start.3
Sparse Core Ops, SparseCore 0:
  10.1 66.3 all-gather.4
  114.2 66.2 all-gather.6
